TPU v7x, 32 devices: a whole 2x2x4 slice. The times are simulated.
32 devices in a mesh: blk: 8 (over z, x), seq: 4 (over y, core).
Axes of the slice: x: 2, y: 2, z: 4, core: 2. Of those that a mesh axis runs over, the one named last changes fastest.
Arguments:
- signal: float32 [32768, 512], P(('blk', 'seq')), may hold values from -6 to 6
- item_start: int32 [32768], P(('blk', 'seq')), may hold values from 0 to 31680, as said below
- frame_slot: int32 [32768], P(('blk', 'seq')), may hold values from 0 to 221, as said below
- mel_frames: float32 [224, 80], P(('blk', 'seq')), may hold values from -6 to 6
- resid_cotan: float32 [32768, 512], P(('blk', 'seq')), may hold values from -6 to 6
- skip_cotan: float32 [32768, 512], P(('blk', 'seq')), may hold values from -6 to 6
- conv_weight: float32 [2, 512, 1024], replicated, may hold values from -0.1875 to 0.1875
- cond_weight: float32 [80, 1024], replicated, may hold values from -0.625 to 0.625
- proj_weight: float32 [512, 1024], replicated, may hold values from -0.75 to 0.75
- biases: float32 [2048], replicated, may hold values from -4 to 4
- conv_moment: float32 [2, 512, 1024], replicated, may hold values from -1792 to 1792
- cond_moment: float32 [80, 1024], replicated, may hold values from -1792 to 1792
- proj_moment: float32 [512, 1024], replicated, may hold values from -384 to 384
- biases_moment: float32 [2048], replicated, may hold values from -1280 to 1280
- conv_average: float32 [2, 512, 1024], replicated, may hold values from -0.1875 to 0.1875
- cond_average: float32 [80, 1024], replicated, may hold values from -0.625 to 0.625
- proj_average: float32 [512, 1024], replicated, may hold values from -0.75 to 0.75
- biases_average: float32 [2048], replicated, may hold values from -4 to 4
Outputs:
- residual: float32 [32768, 512], P(('blk', 'seq'))
- skip_out: float32 [32768, 512], P(('blk', 'seq'))
- signal_grad: float32 [32768, 512], P(('blk', 'seq'))
- mel_grad: float32 [224, 80], P(('blk', 'seq'))
- conv_updated: float32 [2, 512, 1024], replicated
- cond_updated: float32 [80, 1024], replicated
- proj_updated: float32 [512, 1024], replicated
- biases_updated: float32 [2048], replicated
- conv_moment_new: float32 [2, 512, 1024], replicated
- cond_moment_new: float32 [80, 1024], replicated
- proj_moment_new: float32 [512, 1024], replicated
- biases_moment_new: float32 [2048], replicated
- conv_average_new: float32 [2, 512, 1024], replicated
- cond_average_new: float32 [80, 1024], replicated
- proj_average_new: float32 [512, 1024], replicated
- biases_average_new: float32 [2048], replicated
- conv_copy: bfloat16 [2, 512, 1024], replicated
- cond_copy: bfloat16 [80, 1024], replicated
- proj_copy: bfloat16 [512, 1024], replicated
- biases_copy: bfloat16 [2048], replicated
Inputs may be any that keep to these rules, and one draw needn't show every extreme that they name: `item_start`: each clip holds a whole number of mel frames of 200 or 300 samples and at least 1024 samples, except the last two clips, which may be cut short; the last clip begins at sample 32768 - 1088 with frames of 200 samples. This is the first sample of the sample's clip. `frame_slot`: frames are stored 7 slots to each block of 1024 samples, in the block that holds the frame's first sample, in order of time; a sample's frame lies in the sample's own block or in the block before it. Slots that no sample names hold unused values.
All inputs are finite; a program needn't handle non-finite values.
Results may differ from a plain program's by a relative error of at most 0.001.
Values sent between devices are 32-bit elements; how exact they have to be, the bound alone decides.
No kernel may reach another device: no remote copies, remote signals or barrier semaphores. Data moves between devices by JAX's collectives and lax.ppermute only.
A program may use at most 128 MiB of HBM per device.

v0:
```python
import math

import jax
import jax.numpy as jnp
from jax import lax
from jax.experimental import pallas as pl
from jax.experimental.pallas import tpu as pltpu
from jax.sharding import PartitionSpec as P

RESID = 512
GATE = 1024
MELS = 80
DILATION = 64
HALF = 512

f32 = jnp.float32
bf16 = jnp.bfloat16
momentum_rate = 0.9
ema_decay = 0.5
step_scale = 0.15
axes = ("blk", "seq")

VMEM = pl.BlockSpec(memory_space=pltpu.VMEM)
HBM = pl.BlockSpec(memory_space=pltpu.HBM)
ANY = pl.BlockSpec(memory_space=pl.ANY)
MIB = 1 << 20


TOKEN = ((8, 128), f32)

RATE = 3.2e9
TIMES = {
    "pack": 1, "late_gates": 8, "early_gates": 6, "proj_grad_send": 1.8, "gate_grad": 5.8,
    "tap0_send": 1.8, "tap0_keep_tap1_send": 4.5, "tap1_keep": 1.8, "mix": 2.8, "signal_grad": 4.4,
    "back": 1.4, "update1_few": 2, "update1": 1.4, "update2": 2, "update3": 2.7, "update4": 3.3,
}
FOLD = 0.1


def expected(name):
    for key in sorted(TIMES, key=len, reverse=True):
        if key in name:
            return TIMES[key]
    return FOLD


class Order:
    def __init__(self):
        self.last = None

    def call(
        self, body, name, ins, outs, specs=None, out_specs=None, scratch=(), limit=16, aliases=None
    ):
        specs = list(specs) if specs else [VMEM] * len(ins)
        ins = [
            pltpu.with_memory_space_constraint(x, pltpu.HBM) if s is HBM else x
            for x, s in zip(ins, specs)
        ]
        out_specs = list(out_specs) if out_specs else [VMEM] * len(outs)
        after = [] if self.last is None else [self.last]
        n_in, n_after, n_out = len(ins), len(after), len(outs)

        def run(*refs):
            outs = refs[n_in + n_after : n_in + n_after + n_out]
            token = refs[n_in + n_after + n_out]
            token[...] = jnp.zeros(token.shape, f32)
            body(*refs[:n_in], *outs, *refs[n_in + n_after + n_out + 1 :])

        kinds = {id(VMEM): pltpu.VMEM, id(HBM): pltpu.HBM}
        *result, self.last = pl.pallas_call(
            run,
            out_shape=[kinds[id(s)](*o) for o, s in zip(outs, out_specs)] + [pltpu.VMEM(*TOKEN)],
            in_specs=specs + [VMEM] * n_after,
            out_specs=out_specs + [VMEM],
            scratch_shapes=list(scratch),
            input_output_aliases=aliases or {},
            compiler_params=pltpu.CompilerParams(vmem_limit_bytes=limit * MIB),
            cost_estimate=pl.CostEstimate(
                flops=int(RATE * expected(name)), bytes_accessed=1, transcendentals=0
            ),
            name=name,
        )(*ins, *after)
        return result


wide8 = jnp.float8_e5m2
fine8 = jnp.float8_e4m3fn
SIGNAL_SCALE, CONV_SCALE, GRAD_SCALE = 2.0**12, 2.0**18, 2.0**3
UP_SCALE, PROJ_SCALE, GATED_SCALE = 2.0**6, 2.0**9, 2.0**8
LOW = 256.0


def split(x):
    high = x.astype(bf16)
    return high, (x - high.astype(f32)).astype(bf16)


def put(refs, where, x, scale):
    high = x.astype(bf16)
    refs[0][where] = high
    refs[1][where] = (high * bf16(scale)).astype(refs[1].dtype)
    refs[2][where] = ((x - high.astype(f32)) * (scale * LOW)).astype(refs[2].dtype)


def dot(left, right, over):
    return lax.dot_general(left, right, (over, ((), ())), preferred_element_type=f32)


def product(left, right, over, scale):
    axis = [o[0] for o in over]
    low = jnp.concatenate([left[2], left[1]], axis[0])
    high = jnp.concatenate([right[1], right[2]], axis[1])
    return dot(left[0], right[0], over) + dot(low, high, over) * (1.0 / (LOW * scale))


def exact(left, right, over):
    return lax.dot_general(
        left, right, (over, ((), ())), preferred_element_type=f32, precision=lax.Precision.HIGHEST
    )


NN = ((1,), (0,))
NT = ((1,), (1,))
TN = ((0,), (0,))


ORDERS = {
    "proj": ((2, 1, 3, 4), (1, 2, 4, 3)),
    "tap0": ((2, 3, 1, 4), (1, 4, 2, 3)),
    "tap1": ((2, 1, 3, 4), (1, 2, 4, 3)),
}
LARGE = ((6, 0, 3, 7, 1, 4, 5), (0, 6, 3, 1, 7, 4, 5))


def plan(blk, seq, name):
    if (blk, seq) == (8, 4):
        return 0, ORDERS[name]
    if (blk, seq) == (64, 4):
        return 2, LARGE
    rest = tuple(range(1, (blk * seq).bit_length() - 1))
    return 0, (rest, rest)


class Pairs:
    def __init__(self, name):
        blk, seq = lax.axis_size("blk"), lax.axis_size("seq")
        self.count = blk * seq
        self.core_bit, (first, second) = plan(blk, seq, name)
        self.places = [(self.core_bit, self.core_bit), *zip(first, second)]
        self.steps = len(self.places)
        self.pairs = [
            [(i, i ^ (1 << p[(i >> self.core_bit) & 1])) for i in range(self.count)]
            for p in self.places
        ]

    def bit(self, step, sibling=False):
        me = lax.axis_index(axes)
        core = (me >> self.core_bit) & 1
        if sibling:
            core = 1 - core
        if step == 0:
            return core
        a, b = self.places[step]
        return jnp.where(core == 0, (me >> a) & 1, (me >> b) & 1)

    def quarter(self, k):
        core, bit = self.bit(0), self.bit(1, k % 2 == 1)
        return (1 - core if k % 2 else core) * 2 + (1 - bit if k >= 2 else bit)

    def swap(self, x, step):
        return lax.ppermute(x, axes, self.pairs[step])


class Sum:
    def __init__(self, order, pairs, name, send, whole=1):
        self.order, self.pairs, self.name = order, pairs, name
        self.parted = pairs.steps - whole
        self.step, self.back = 0, False
        self.got = pairs.swap(send, 0)
        self.done = False

    def advance(self):
        if self.done:
            return
        pairs, step = self.pairs, self.step
        label = f"{self.name}_{'join' if self.back else 'fold'}{step}"
        if self.back:
            size = self.piece.shape[0]

            def body(mine, got, out):
                bit = pairs.bit(step)
                out[pl.ds(bit * size, size)] = mine[...]
                out[pl.ds((1 - bit) * size, size)] = got[...]

            (self.piece,) = self.order.call(
                body, label, [self.piece, self.got], [((2 * size, 8, 128), f32)]
            )
            self.step -= 1
        elif step + 1 < self.parted:
            half = self.rest.shape[0] // 2

            def body(keep, got, send, rest):
                bit = pairs.bit(step + 1)
                here, there = pl.ds(bit * half, half), pl.ds((1 - bit) * half, half)
                send[...] = keep[there] + got[there]
                rest[...] = keep[here] + got[here]

            shape = ((half, 8, 128), f32)
            send, self.rest = self.order.call(body, label, [self.rest, self.got], [shape, shape])
            self.step += 1
            self.got = pairs.swap(send, self.step)
            return
        else:
            mine = self.rest if step < self.parted else self.piece

            def body(mine, got, out):
                out[...] = mine[...] + got[...]

            (self.piece,) = self.order.call(body, label, [mine, self.got], [(mine.shape, f32)])
            self.step += 1
            if self.step == pairs.steps:
                self.back, self.step = True, self.parted - 1
        if self.back and self.step == 1:
            self.done = True
            return
        self.got = pairs.swap(self.piece, self.step)


def pack_body(rows, signal, mel, out, frames, sem):
    copy = pltpu.make_async_copy(
        signal.at[pl.ds(rows - DILATION, DILATION)], out.at[pl.ds(0, DILATION)], sem.at[0]
    )
    other = pltpu.make_async_copy(mel, frames, sem.at[1])
    copy.start()
    other.start()
    out[DILATION:, :] = jnp.zeros((8, RESID), f32)
    other.wait()
    out[DILATION : DILATION + mel.shape[0], :MELS] = frames[...]
    copy.wait()


def columns(row, rows):
    return jnp.transpose(jnp.broadcast_to(row, (8, rows)))[:, :1]


def picks(slots, part, slot_count, sel):
    me = lax.axis_index(axes)
    local = (slots[:, part * HALF : (part + 1) * HALF] - (me - 1) * slot_count).astype(f32)
    local = columns(local, HALF).astype(jnp.int32)
    lane = lax.broadcasted_iota(jnp.int32, (HALF, 128), 1)
    hot = (lane == local) | (lane == local + 16) | (lane == 15)
    sel[...] = jnp.where(hot, 1.0, 0.0).astype(bf16)


def usable_row(starts, first, count, row_count):
    time = lax.axis_index(axes) * row_count + first + lax.broadcasted_iota(jnp.int32, (1, count), 1)
    return jnp.where(time - DILATION >= starts[:, first : first + count], 1.0, 0.0)


def frame_terms(mel, prior, cond, bias, table, frames):
    slot_count = mel.shape[0]
    frames[...] = jnp.zeros((16, 128), f32)
    frames[slot_count : 2 * slot_count, :MELS] = mel[...]
    if prior is not None:
        frames[:slot_count, :MELS] = prior
    row = jnp.concatenate([bias[i : i + 1, :] for i in range(8)], 1)
    terms = exact(frames[:, :MELS], cond[...], NN) + row
    keep = lax.broadcasted_iota(jnp.int32, (16, GATE), 0) < 2 * slot_count
    high, low = split(jnp.where(keep, terms, 0.0))
    table[...] = jnp.zeros((128, GATE), bf16)
    table[0:16, :] = high
    table[16:32, :] = low


def gates(tanh_in, sigm_in, cols, g, ca, cb):
    th = jnp.tanh(tanh_in)
    sg = 0.5 * jnp.tanh(0.5 * sigm_in) + 0.5
    gated = th * sg
    put(g, (slice(None), cols), gated, GATED_SCALE)
    ca[:, cols] = sg * (1.0 - th * th)
    cb[:, cols] = gated * (1.0 - sg)


def preact_block(d, x, sel, w, table, cols):
    main = dot(
        jnp.concatenate([d[0][...], x[0][...], sel[...]], 1),
        jnp.concatenate([w[0][:, cols], table[:, cols]], 0),
        NN,
    )
    low = dot(
        jnp.concatenate([d[2][...], x[2][...], d[1][...], x[1][...]], 1),
        jnp.concatenate([w[1][:, cols], w[2][:, cols]], 0),
        NN,
    )
    return main + low * (1.0 / (LOW * SIGNAL_SCALE * CONV_SCALE))


BLOCK = 256


def late_body(rows, *refs):
    signal, conv, cond, mel, slots, starts, bias = refs[:7]
    far, near, (table, frames, sem) = refs[7:10], refs[28:31], refs[31:]
    x0, x1, d, w = (refs[i : i + 3] for i in (10, 13, 16, 19))
    sel, g, ca, cb = refs[22], refs[23:26], refs[26], refs[27]
    copies = [pltpu.make_async_copy(a, b, sem.at[i]) for i, (a, b) in enumerate(zip(far, near))]
    for copy in copies:
        copy.start()
    first = HALF - DILATION
    picks(slots, 1, mel.shape[0], sel)
    frame_terms(mel, None, cond, bias, table, frames)
    usable = columns(usable_row(starts, HALF, HALF, rows), HALF)
    put(x1, slice(None), signal[HALF:, :], SIGNAL_SCALE)
    put(d, slice(None), signal[first : first + HALF, :] * usable, SIGNAL_SCALE)
    for j in range(HALF // BLOCK):
        blocks = [slice(c + j * BLOCK, c + (j + 1) * BLOCK) for c in (0, HALF)]
        products = []
        for cols in blocks:
            for tap in range(2):
                span = slice(tap * RESID, (tap + 1) * RESID)
                put(w, (span, cols), conv[tap, :, cols], CONV_SCALE)
            products.append(preact_block(d, x1, sel, w, table, cols))
        gates(*products, blocks[0], g, ca, cb)
    put(x0, slice(None), signal[0:HALF, :], SIGNAL_SCALE)
    for copy in copies:
        copy.wait()


def early_body(rows, *refs):
    halo, signal = refs[:2]
    x, w = refs[2:5], refs[5:8]
    cond, mel, slots, starts, bias, resid_cotan, skip_cotan, proj = refs[8:16]
    d, sel, g, ca, cb = refs[16:19], refs[19], refs[20:23], refs[23], refs[24]
    u, p, usum, table, frames = refs[25:28], refs[28:31], *refs[31:]
    picks(slots, 0, mel.shape[0], sel)
    frame_terms(mel, halo[DILATION : DILATION + mel.shape[0], :MELS], cond, bias, table, frames)
    usable = columns(usable_row(starts, 0, HALF, rows), HALF)
    put(d, slice(0, DILATION), halo[0:DILATION, :] * usable[0:DILATION], SIGNAL_SCALE)
    rest = HALF - DILATION
    put(d, slice(DILATION, None), signal[0:rest, :] * usable[DILATION:], SIGNAL_SCALE)
    usum[...] = jnp.zeros((8, 2 * RESID), f32)

    def part_cotangents(first, count):
        for r in range(first, first + count, 128):
            for k, part in enumerate((resid_cotan, skip_cotan)):
                span = slice(k * RESID, (k + 1) * RESID)
                value = part[r : r + 128, :]
                put(u, (slice(r, r + 128), span), value, UP_SCALE)
                usum[:, span] += jnp.sum(value.reshape(16, 8, RESID), 0)

    for j in range(HALF // BLOCK):
        tc, sc = (slice(c + j * BLOCK, c + (j + 1) * BLOCK) for c in (0, HALF))
        tanh_in = preact_block(d, x, sel, w, table, tc)
        part_cotangents(j * rows // 2, rows // 4)
        sigm_in = preact_block(d, x, sel, w, table, sc)
        part_cotangents(j * rows // 2 + rows // 4, rows // 4)
        gates(tanh_in, sigm_in, tc, g, ca, cb)
    put(p, slice(None), proj[...], PROJ_SCALE)


def put_tiles(out, value, col0, stride=None):
    height, width = value.shape
    for r in range(height // 8):
        base = r * 8 if stride is None else (r * 8 // QUARTER) * stride + (r * 8) % QUARTER
        for c in range(width // 128):
            out[base + col0 // 128 + c] = value[8 * r : 8 * r + 8, 128 * c : 128 * c + 128]


WIDE = 512


def weight_grad(left, cols, right, out, scale, stride=None):
    left = [jnp.concatenate([a[:, cols], b[:, cols]], 0) for a, b in zip(left[:3], left[3:])]
    for c in range(0, GATE, WIDE):
        wide = [r[:, c : c + WIDE] for r in right]
        put_tiles(out, product(left, wide, TN, scale), c, stride)


QUARTER = 128


def solve(pairs, args):
    (
        signal, item_start, frame_slot, mel_frames, resid_cotan, skip_cotan,
        conv_weight, cond_weight, proj_weight, biases,
        conv_moment, cond_moment, proj_moment, biases_moment,
        conv_average, cond_average, proj_average, biases_average,
    ) = args
    rows = signal.shape[0]
    slot_count = mel_frames.shape[0]
    slots = frame_slot.reshape(1, rows)
    starts = item_start.reshape(1, rows)
    bias = biases.reshape(16, 128)
    count = pairs.count
    order = Order()
    call = order.call

    def core_half(own):
        bit = pairs.bit(0)
        return bit if own else 1 - bit

    def half_cols(own):
        return pl.ds(pl.multiple_of(core_half(own) * 2 * QUARTER, 2 * QUARTER), 2 * QUARTER)

    (packed,) = call(
        lambda *r: pack_body(rows, *r), "pack", [signal, mel_frames],
        [((DILATION + 8, RESID), f32)], specs=[HBM, HBM],
        scratch=[pltpu.VMEM((slot_count, MELS), f32), pltpu.SemaphoreType.DMA((2,))],
    )
    halo = lax.ppermute(packed, axes, [(i, i + 1) for i in range(count - 1)])

    wide, fine = (bf16, wide8, wide8), (bf16, fine8, fine8)
    half = [((HALF, RESID), t) for t in wide]
    half_gate = [((HALF, RESID), t) for t in fine]
    half32 = ((HALF, HALF), f32)
    square = [((GATE, GATE), t) for t in wide]
    pick = ((HALF, 128), bf16)
    small_scratch = [pltpu.VMEM((128, GATE), bf16), pltpu.VMEM((16, 128), f32)]
    held = [resid_cotan, skip_cotan, proj_weight]
    out = call(
        lambda *r: late_body(rows, *r), "late_gates",
        [signal, conv_weight, cond_weight, mel_frames, slots, starts, bias, *held],
        [*half, *half, *half, *square, pick, *half_gate, half32, half32, *((x.shape, x.dtype) for x in held)],
        specs=[VMEM] * 7 + [HBM] * 3,
        scratch=[*small_scratch, pltpu.SemaphoreType.DMA((3,))],
    )
    x0, x1, d1, w = (out[i : i + 3] for i in (0, 3, 6, 9))
    sel1, g1, ca1, cb1, (resid_in, skip_in, proj_in) = out[12], out[13:16], out[16], out[17], out[18:]
    out = call(
        lambda *r: early_body(rows, *r), "early_gates",
        [halo, signal, *x0, *w, cond_weight, mel_frames, slots, starts, bias, resid_in, skip_in, proj_in],
        [*half, pick, *half_gate, half32, half32, *(((GATE, GATE), t) for t in fine),
         *(((HALF, GATE), t) for t in fine), ((8, GATE), f32)],
        scratch=small_scratch,
    )
    d0, sel0, g0, ca0, cb0 = out[0:3], out[3], out[4:7], out[7], out[8]
    u, p, usum = out[9:12], out[12:15], out[15]

    tiles = ((2 * QUARTER, 8, 128), f32)

    def proj_half(own):
        def body(*refs):
            weight_grad(refs[:6], half_cols(own), refs[6:9], refs[9], GATED_SCALE * UP_SCALE)

        return body

    gated = [*g0, *g1, *u]
    (proj_send,) = call(proj_half(False), "proj_grad_send", gated, [tiles])
    proj_sum = Sum(order, pairs, "proj", proj_send, WHOLE[0])

    def gate_grad(*refs):
        u, p, (ca0, ca1, cb0, cb1) = refs[6:9], refs[9:12], refs[12:16]
        out, gp = refs[16], refs[17:20]
        proj_half(True)(*refs[:9], out)
        right = [x[...] for x in p]
        for r in range(0, rows, BLOCK):
            span = slice(r, r + BLOCK)
            grad = product([x[span, :] for x in u], right, NT, UP_SCALE * PROJ_SCALE)
            ca, cb = (ca0, cb0) if r < HALF else (ca1, cb1)
            inner = slice(r % HALF, r % HALF + BLOCK)
            put(gp, (span, slice(0, HALF)), grad * ca[inner, :], GRAD_SCALE)
            put(gp, (span, slice(HALF, GATE)), grad * cb[inner, :], GRAD_SCALE)

    proj_sum.rest, *gp = call(
        gate_grad, "gate_grad", [*gated, *p, ca0, ca1, cb0, cb1], [tiles, *square]
    )
    proj_sum.advance()

    def tap_half(own, stride=None):
        def body(*refs):
            weight_grad(
                refs[:6], half_cols(own), refs[6:9], refs[9], SIGNAL_SCALE * GRAD_SCALE, stride
            )

        return body

    (send,) = call(tap_half(False), "tap0_send", [*d0, *d1, *gp], [tiles])
    tap0_sum = Sum(order, Pairs("tap0"), "tap0", send, WHOLE[1])

    few = 24
    while (QUARTER + few) % max(1, count // 4):
        few += 8
    quarter = QUARTER + few
    wide_tiles = ((2 * quarter, 8, 128), f32)

    def tap1_half(own, *refs):
        both, out = refs[9:]
        tap_half(own, quarter)(*refs[:9], out)
        for q in range(2):
            out[pl.ds(q * quarter + QUARTER, few)] = both[core_half(own) * 2 + q]

    def tap0_keep_tap1_send(*refs):
        d, x, gp, (sel0, sel1, usum, mel, halo) = refs[:6], refs[6:12], refs[12:15], refs[15:20]
        zero_keep, one_send, both, frame_grad, frames = refs[20:]
        tap_half(True)(*d, *gp, zero_keep)
        sel = jnp.concatenate([sel0[:, 0:16], sel1[:, 0:16]], 0)
        found = dot(sel, gp[0][...], TN)
        found += dot(sel.astype(wide8), gp[2][...], TN) * (1.0 / (LOW * GRAD_SCALE))
        frame_grad[...] = found
        frames[...] = jnp.zeros((16, 128), f32)
        frames[:slot_count, :MELS] = halo[DILATION : DILATION + slot_count, :MELS]
        frames[slot_count : 2 * slot_count, :MELS] = mel[...]
        cond_grad = exact(frames[:, :MELS], found, TN)
        both[...] = jnp.zeros((4, few, 8, 128), f32)
        for q in range(4):
            part = cond_grad[24 * q : min(24 * q + 24, MELS), :]
            put_tiles(both.at[q], part, 0)
        sums = jnp.sum(usum[...], 0, keepdims=True)
        for i in range(8):
            lane = slice(128 * i, 128 * i + 128)
            both[3, 8, i : i + 1, :] = found[15:16, lane]
            both[3, 9, i : i + 1, :] = sums[:, lane]
        tap1_half(False, *x, *gp, both, one_send)

    tap0_sum.rest, send, few_grad, frame_grad = call(
        tap0_keep_tap1_send, "tap0_keep_tap1_send",
        [*d0, *d1, *x0, *x1, *gp, sel0, sel1, usum, mel_frames, halo],
        [tiles, wide_tiles, ((4, few, 8, 128), f32), ((16, GATE), f32)],
        scratch=[pltpu.VMEM((16, 128), f32)],
    )
    tap1_sum = Sum(order, Pairs("tap1"), "tap1", send, WHOLE[2])
    tap0_sum.advance()
    (tap1_sum.rest,) = call(
        lambda *r: tap1_half(True, *r), "tap1_keep", [*x0, *x1, *gp, few_grad], [wide_tiles]
    )

    def tap_back(gp, w, rows_, tap):
        span = slice(tap * RESID, (tap + 1) * RESID)
        return product(
            [x[rows_, :] for x in gp], [x[span, :] for x in w], NT, GRAD_SCALE * CONV_SCALE
        )

    def back_body(*refs):
        gp, w, (frame_grad, cond, starts, out, own) = refs[:3], refs[3:6], refs[6:]
        usable = columns(usable_row(starts, 0, 128, rows), 128)[0:DILATION]
        out[0:DILATION, :] = tap_back(gp, w, slice(0, DILATION), 0) * usable
        mels = exact(frame_grad[...], cond[...], NT)
        out[DILATION:, :] = jnp.zeros((8, RESID), f32)
        out[DILATION : DILATION + slot_count, :MELS] = mels[:slot_count]
        own[...] = mels[slot_count : 2 * slot_count]

    state = {}

    def back():
        state["back"], state["mel_own"] = call(
            back_body, "back", [*gp, *w, frame_grad, cond_weight, starts],
            [((DILATION + 8, RESID), f32), ((slot_count, MELS), f32)],
        )
        state["came"] = lax.ppermute(state["back"], axes, [(i, i - 1) for i in range(1, count)])

    def mix(r):
        def body(*refs):
            g, p, (bias, signal) = refs[:3], refs[3:6], refs[6:8]
            outs, (held, sem) = refs[-4:-2], refs[-2:]
            copies = []
            for s in range(0, HALF, BLOCK):
                inner = slice(s, s + BLOCK)
                span = slice(r + s, r + s + BLOCK)
                left = [x[inner, :] for x in g]
                for k, c in enumerate((0, RESID)):
                    w = slice(c, c + RESID)
                    first = 8 + c // 128
                    row = jnp.concatenate([bias[i : i + 1, :] for i in range(first, first + 4)], 1)
                    mixed = product(left, [x[:, w] for x in p], NN, GATED_SCALE * PROJ_SCALE) + row
                    held[k, inner, :] = mixed + signal[span, :] if k == 0 else mixed
                    copies.append(
                        pltpu.make_async_copy(
                            held.at[k, pl.ds(s, BLOCK)],
                            outs[k].at[pl.ds(r + s, BLOCK)],
                            sem.at[len(copies)],
                        )
                    )
                    copies[-1].start()
            for copy in copies:
                copy.wait()

        old = state.get("mixed", [])
        state["mixed"] = call(
            body, f"mix{r}", [*(g0 if r < HALF else g1), *p, bias, signal, *old],
            [((rows, RESID), f32)] * 2, aliases={8 + i: i for i in range(len(old))},
            specs=[VMEM] * 8 + [HBM] * len(old), out_specs=[HBM] * 2,
            scratch=[pltpu.VMEM((2, HALF, RESID), f32), pltpu.SemaphoreType.DMA((4,))],
        )

    def signal_grad(r):
        last = r + HALF == rows

        def body(*refs):
            gp, w, (starts, resid_cotan) = refs[:3], refs[3:6], refs[6:8]
            held, mels, sem = refs[-3:]
            copies = []
            if last:
                came, own, _, out, mel_grad = refs[8:-3]
                mels[...] = own[...] + came[DILATION : DILATION + slot_count, :MELS]
                copies.append(pltpu.make_async_copy(mels, mel_grad, sem.at[2]))
                copies[0].start()
            else:
                out = refs[-4]
            usable = columns(usable_row(starts, 0, rows, rows), rows)
            for s in range(r, r + HALF, BLOCK):
                span = slice(s, s + BLOCK)
                ahead = slice(s + DILATION, min(s + DILATION + BLOCK, rows))
                inner = slice(s - r, s - r + BLOCK)
                later = tap_back(gp, w, ahead, 0) * usable[ahead]
                held[inner, :] = tap_back(gp, w, span, 1) + resid_cotan[span, :]
                held[s - r : s - r + later.shape[0], :] += later
                if s + BLOCK == rows:
                    held[HALF - DILATION :, :] += came[0:DILATION, :]
                copies.append(
                    pltpu.make_async_copy(
                        held.at[pl.ds(s - r, BLOCK)], out.at[pl.ds(s, BLOCK)], sem.at[(s - r) // BLOCK]
                    )
                )
                copies[-1].start()
            for copy in copies:
                copy.wait()

        ins = [*gp, *w, starts, resid_in]
        outs = [((rows, RESID), f32)]
        if last:
            ins += [state["came"], state["mel_own"]]
            outs += [((slot_count, MELS), f32)]
        old = state.get("signal_grad", [])
        state["signal_grad"] = call(
            body, f"signal_grad{r}", ins + list(old), outs, aliases={len(ins): 0} if old else {},
            specs=[VMEM] * len(ins) + [HBM] * len(old), out_specs=[HBM] * len(outs),
            scratch=[pltpu.VMEM((HALF, RESID), f32), pltpu.VMEM((slot_count, MELS), f32),
                     pltpu.SemaphoreType.DMA((3,))],
        )

    root = math.sqrt(rows * count)
    conv_rate = step_scale / (math.sqrt(2 * RESID) * 1.5 * root)
    cond_rate = step_scale / (math.sqrt(MELS) * 1.5 * root)
    proj_rate = step_scale / (math.sqrt(GATE // 16) * 0.3 * root)
    biases_rate = step_scale * 0.3 / (1.2 * root)

    def step_tile(g, w, m, a, rate):
        m = momentum_rate * m + g
        w = w - rate * (g + momentum_rate * m)
        return w, m, ema_decay * a + (1.0 - ema_decay) * w

    conv = (conv_weight, conv_moment, conv_average)
    matrices = {
        "proj": ((proj_weight, proj_moment, proj_average), proj_rate),
        "conv": (conv, conv_rate),
    }
    kinds = (f32, f32, f32, bf16)
    few_args = (cond_weight, cond_moment, cond_average, bias,
                biases_moment.reshape(16, 128), biases_average.reshape(16, 128))
    few_shapes = [((MELS, GATE), t) for t in kinds] + [((16, 128), t) for t in kinds]

    def update_few(pieces, ins, outs, held, grads, sem):
        for k, piece in enumerate(pieces):
            first = tap1_sum.pairs.quarter(k) * 24
            grads[pl.ds(first, 24)] = piece[QUARTER : QUARTER + 24]
        for r in range(0, MELS, 16):
            span = slice(r, r + 16)
            for c in range(0, GATE, 128):
                w = slice(c, c + 128)
                tile = r + c // 128
                g = jnp.concatenate([grads[tile], grads[tile + 8]], 0)
                new = step_tile(g, *(x[span, w] for x in ins[:3]), cond_rate)
                for ref, value in zip(held, new):
                    ref[span, w] = value
                held[3][span, w] = new[0].astype(bf16)
        grad = jnp.concatenate([grads[MELS], grads[MELS + 1]], 0)
        new = step_tile(grad, *(x[...] for x in ins[3:]), biases_rate)
        for ref, value in zip(held[4:], new):
            ref[...] = value
        held[7][...] = new[0].astype(bf16)
        copies = [
            pltpu.make_async_copy(a, b, sem.at[i]) for i, (a, b) in enumerate(zip(held, outs))
        ]
        for copy in copies:
            copy.start()
        return copies

    def update(key, items, few_too=False):
        trio, rate = matrices[key]
        old = state.get(key, [])
        n = len(items)
        ins = [total.pieces[k] for total, k, _ in items] + [*trio]
        if few_too:
            ins += [*tap1_sum.pieces, *few_args]

        def body(*refs):
            refs = list(refs)
            take = lambda count: [refs.pop(0) for _ in range(count)]
            gs, trio_refs = take(n), take(3)
            few_refs = take(10) if few_too else []
            take(len(old))
            outs = take(4)
            few_outs = take(8) if few_too else []
            held, sem = take(4), refs.pop(0)
            copies = []
            if few_too:
                copies += update_few(
                    few_refs[:4], few_refs[4:], few_outs, refs[:8], refs[8], refs[9]
                )
            for i, (total, k, lead) in enumerate(items):
                first = pl.multiple_of(total.pairs.quarter(k) * QUARTER, QUARTER)
                parts = [x if lead is None else x.at[lead] for x in (*trio_refs, *outs)]
                for r in range(0, QUARTER, 16):
                    span = slice(i * QUARTER + r, i * QUARTER + r + 16)
                    there = pl.ds(first + r, 16)
                    for c in range(0, GATE, 128):
                        w = slice(c, c + 128)
                        tile = r + c // 128
                        g = jnp.concatenate([gs[i][tile], gs[i][tile + 8]], 0)
                        new = step_tile(g, *(x[there, w] for x in parts[:3]), rate)
                        for ref, value in zip(held, new):
                            ref[span, w] = value
                        held[3][span, w] = new[0].astype(bf16)
                for o in range(4):
                    copies.append(
                        pltpu.make_async_copy(
                            held[o].at[pl.ds(i * QUARTER, QUARTER)],
                            parts[3 + o].at[pl.ds(first, QUARTER)],
                            sem.at[i * 4 + o],
                        )
                    )
                    copies[-1].start()
            for copy in copies:
                copy.wait()

        scratch = [pltpu.VMEM((n * QUARTER, GATE), t) for t in kinds]
        scratch += [pltpu.SemaphoreType.DMA((4 * n,))]
        if few_too:
            scratch += [pltpu.VMEM(*x) for x in few_shapes]
            scratch += [pltpu.VMEM((96, 8, 128), f32), pltpu.SemaphoreType.DMA((8,))]
        result = call(
            body, f"{key}_update{n}" + ("_few" if few_too else ""), [*ins, *old],
            [(trio[0].shape, t) for t in kinds] + (few_shapes if few_too else []),
            specs=[VMEM] * len(ins) + [HBM] * len(old),
            out_specs=[HBM] * (12 if few_too else 4), scratch=scratch,
            aliases={len(ins) + i: i for i in range(len(old))},
        )
        state[key] = result[:4]
        if few_too:
            state["few"] = result[4:]

    def spread(total):
        while not total.done:
            total.advance()
        total.pieces = [total.piece, total.pairs.swap(total.piece, 0), total.pairs.swap(total.piece, 1)]

    def relay(total):
        total.pieces.append(total.pairs.swap(total.pieces[2], 0))

    trees = {"P": (proj_sum, "proj", None), "0": (tap0_sum, "conv", 0), "1": (tap1_sum, "conv", 1)}
    fill = {"back": back}
    for i in range(2):
        fill[f"mix{i}"] = lambda i=i: mix(i * HALF)
        fill[f"sg{i}"] = lambda i=i: signal_grad(i * HALF)
    for word in SCRIPT.split():
        if word in trees:
            trees[word][0].advance()
        elif word in fill:
            fill[word]()
        elif word[0] == "s":
            spread(trees[word[1]][0])
        elif word[0] == "r":
            relay(trees[word[1]][0])
        else:
            items, name = [], None
            for letter in word[1:]:
                if letter in trees:
                    name = letter
                elif letter in "abcd":
                    total, key, lead = trees[name]
                    items.append((total, "abcd".index(letter), lead))
            update(key, items, "f" in word)
    proj_new, conv_new = state["proj"], state["conv"]
    cond_new, bias_new = state["few"][:4], [x.reshape(-1) for x in state["few"][4:]]
    result = [*state["mixed"], *state["signal_grad"]]
    for k in range(4):
        result += [conv_new[k], cond_new[k], proj_new[k], bias_new[k]]
    return tuple(result)


WHOLE = (2, 1, 1)
SCRIPT = """
P sg0 P 1 back 0 mix0 P 1 mix1 0 1 P 0 1 P 0 1 0 sP rP 1 sg1 0 s0 1 s1 =0a =Pab r0 =Pd =Pc r1 =0cd1c =1b =0b1adf
"""


def shards(*args):
    return solve(Pairs("proj"), args)


def solution(mesh):
    rows = P(("blk", "seq"), None)
    in_specs = (rows, P(("blk", "seq")), P(("blk", "seq")), rows, rows, rows) + (P(),) * 12
    out_specs = (rows,) * 4 + (P(),) * 16
    return jax.shard_map(shards, mesh=mesh, in_specs=in_specs, out_specs=out_specs, check_vma=False)
```

profile of v0, /device:TPU:0, one launch (start us, length us, event | category | flops | bytes accessed | tf_op | source)
XLA Modules:
  0.0 120.1 jit_solution(7013346225588134280)
XLA Ops:
  1.8 2.6 %collective-permute-start = (f32[72,512]{1,0:T(8,128)S(1)}, f32[72,512]{1,0:T(8,128)S(1)}, u32[]{:S(2)}, u32[]{:S(2)}) collective-permute-start(f32[72,512]{1,0:T(8,128)S(1)} %get-tuple-element.185), channel_id=1, source_target_pairs={{0,1},{1,2},{2,3},{3,4},{4,5},{5,6},{6,7},{7,8},{8,9},{9,10},{10,1... | collective-permute-start | bytes 442376 | tf_op jit(solution)/shard_map/ppermute | solution.py:410
  4.5 6.4 %late_gates.1 = (bf16[512,512]{1,0:T(8,128)(2,1)S(1)}, f8e5m2[512,512]{1,0:T(32,128)(4,1)S(1)}, f8e5m2[512,512]{1,0:T(32,128)(4,1)S(1)}, bf16[512,512]{1,0:T(8,1...) custom-call(f32[1024,512]{1,0:T(8,128)S(1)} %copy-done.9, ...), custom_call_target="tpu_custom_call" | custom-call | flops 25600000000 | bytes 1 | tf_op jit(solution)/shard_map/late_gates/pallas_call | solution.py:70
  10.9 5.0 %early_gates.1 = (bf16[512,512]{1,0:T(8,128)(2,1)S(1)}, f8e5m2[512,512]{1,0:T(32,128)(4,1)S(1)}, f8e5m2[512,512]{1,0:T(32,128)(4,1)S(1)}, bf16[512,128]{1,0:T(8,...) custom-call(f32[72,512]{1,0:T(8,128)S(1)} %collective-permute-done.r, ...), custom_call_target="tpu_custom_call" | custom-call | flops 19200000000 | bytes 1 | tf_op jit(solution)/shard_map/early_gates/pallas_call | solution.py:70
  17.3 2.7 %collective-permute-start.1 = (f32[256,8,128]{2,1,0:T(8,128)S(1)}, f32[256,8,128]{2,1,0:T(8,128)S(1)}, u32[]{:S(2)}, u32[]{:S(2)}) collective-permute-start(f32[256,8,128]{2,1,0:T(8,128)S(1)} %get-tuple-element.227), channel_id=1, source_target_pairs={{0,1},{1,0},{2,3},{3,2},{4,5},{5,4},{6,7},{7,6},{8,9},{9,8},{10,11... | collective-permute-start | bytes 3145736 | tf_op jit(solution)/shard_map/ppermute | solution.py:171
  20.0 4.7 %gate_grad.1 = (f32[256,8,128]{2,1,0:T(8,128)S(1)}, bf16[1024,1024]{1,0:T(8,128)(2,1)S(1)}, f8e5m2[1024,1024]{1,0:T(32,128)(4,1)S(1)}, f8e5m2[1024,1024]{1,0:T(32,128)(4,1)S(1)}, f32[8,128]{1,0:T(8,128)S(1)}) custom-call(bf16[512,512]{1,0:T(8,128)(2,1)S(1)} %get-tuple-element.199.refs_0_, f8e4m3fn[512,512]{1,0:T(32,128)(4,1)S(1)} %get-tuple-element.200.refs_1_, ...), custom_call_target="tpu_custom_call" | custom-call | flops 18560000000 | bytes 1 | tf_op jit(solution)/shard_map/gate_grad/pallas_call | solution.py:70
  27.8 3.2 %tap0_keep_tap1_send.1 = (f32[256,8,128]{2,1,0:T(8,128)S(1)}, f32[304,8,128]{2,1,0:T(8,128)S(1)}, f32[4,24,8,128]{3,2,1,0:T(8,128)S(1)}, f32[16,1024]{1,0:T(8,128)S(1)}, f32[8,128]{1,0:T(8,128)S(1)}) custom-call(bf16[512,512]{1,0:T(8,128)(2,1)S(1)} %get-tuple-element.202.refs_0_, f8e5m2[512,512]{1,0:T(32,128)(4,1)S(1)} %get-tuple-element.203.refs_1_, ...), custom_call_target="tpu_custom_call" | custom-call | flops 14400000000 | bytes 1 | tf_op jit(solution)/shard_map/tap0_keep_tap1_send/pallas_call | solution.py:70
  37.2 3.5 %signal_grad0.1 = (f32[1024,512]{1,0:T(8,128)}, f32[8,128]{1,0:T(8,128)S(1)}) custom-call(bf16[1024,1024]{1,0:T(8,128)(2,1)S(1)} %get-tuple-element.220.refs_6_.refs_12_.refs_0_, f8e5m2[1024,1024]{1,0:T(32,128)(4,1)S(1)} %get-tuple-element.221.refs_7_.refs_13_.refs_1_, f8e5m2[1024,1024]{1,0:T(32,128)(4,1)S(1)} %get-tuple-element.222.refs_8_.refs_14_.refs_2_, ...), custom_call_target="tpu_custom_call" | custom-call | flops 14080000000 | bytes 1 | tf_op jit(solution)/shard_map/signal_grad0/pallas_call | solution.py:70
  40.7 2.7 %collective-permute-done.6.refs_1_ = f32[64,8,128]{2,1,0:T(8,128)S(1)} collective-permute-done((f32[64,8,128]{2,1,0:T(8,128)S(1)}, f32[64,8,128]{2,1,0:T(8,128)S(1)}, u32[]{:S(2)}, u32[]{:S(2)}) %collective-permute-start.6) | collective-permute-done | bytes 262176 | tf_op jit(solution)/shard_map/ppermute | solution.py:171
  48.4 2.2 %mix0.1 = (f32[1024,512]{1,0:T(8,128)}, f32[1024,512]{1,0:T(8,128)}, f32[8,128]{1,0:T(8,128)S(1)}) custom-call(bf16[512,512]{1,0:T(8,128)(2,1)S(1)} %get-tuple-element.199.refs_0_, f8e4m3fn[512,512]{1,0:T(32,128)(4,1)S(1)} %get-tuple-element.200.refs_1_, f8e4m3fn[512,512]{1,0:T(32,128)(4,1)S(1)} %get-tuple-element.201.refs_2_, ...), custom_call_target="tpu_custom_call" | custom-call | flops 8960000000 | bytes 1 | tf_op jit(solution)/shard_map/mix0/pallas_call | solution.py:70
  50.6 4.4 %collective-permute-done.8.refs_1_ = f32[64,8,128]{2,1,0:T(8,128)S(1)} collective-permute-done((f32[64,8,128]{2,1,0:T(8,128)S(1)}, f32[64,8,128]{2,1,0:T(8,128)S(1)}, u32[]{:S(2)}, u32[]{:S(2)}) %collective-permute-start.8) | collective-permute-done | bytes 262176 | tf_op jit(solution)/shard_map/ppermute | solution.py:171
  56.2 2.9 %collective-permute-start.10 = (f32[76,8,128]{2,1,0:T(8,128)S(1)}, f32[76,8,128]{2,1,0:T(8,128)S(1)}, u32[]{:S(2)}, u32[]{:S(2)}) collective-permute-start(f32[76,8,128]{2,1,0:T(8,128)S(1)} %get-tuple-element.266), channel_id=1, source_target_pairs={{0,2},{1,5},{2,0},{3,7},{4,6},{5,1},{6,4},{7,3},{8,10},{9,13},{10,... | collective-permute-start | bytes 933896 | tf_op jit(solution)/shard_map/ppermute | solution.py:171
  59.0 2.2 %mix512.1 = (f32[1024,512]{1,0:T(8,128)}, f32[1024,512]{1,0:T(8,128)}, f32[8,128]{1,0:T(8,128)S(1)}) custom-call(bf16[512,512]{1,0:T(8,128)(2,1)S(1)} %get-tuple-element.182.refs_3_.refs_0_, f8e4m3fn[512,512]{1,0:T(32,128)(4,1)S(1)} %get-tuple-element.183.refs_4_.refs_1_, ...), custom_call_target="tpu_custom_call", output_to_operand_aliasing={{0}: (8, {}), {1}: (9, {})} | custom-call | flops 8960000000 | bytes 1 | tf_op jit(solution)/shard_map/mix512/pallas_call | solution.py:70
  64.0 2.5 %collective-permute-start.12 = (f32[38,8,128]{2,1,0:T(8,128)S(1)}, f32[38,8,128]{2,1,0:T(8,128)S(1)}, u32[]{:S(2)}, u32[]{:S(2)}) collective-permute-start(f32[38,8,128]{2,1,0:T(8,128)S(1)} %get-tuple-element.272), channel_id=1, source_target_pairs={{0,8},{1,17},{2,10},{3,19},{4,12},{5,21},{6,14},{7,23},{8,0},{9,25... | collective-permute-start | bytes 466952 | tf_op jit(solution)/shard_map/ppermute | solution.py:171
  66.5 2.2 %collective-permute-done.14.refs_1_ = f32[64,8,128]{2,1,0:T(8,128)S(1)} collective-permute-done((f32[64,8,128]{2,1,0:T(8,128)S(1)}, f32[64,8,128]{2,1,0:T(8,128)S(1)}, u32[]{:S(2)}, u32[]{:S(2)}) %collective-permute-start.14) | collective-permute-done | bytes 262176 | tf_op jit(solution)/shard_map/ppermute | solution.py:171
  69.4 2.6 %collective-permute-done.12.refs_1_ = f32[38,8,128]{2,1,0:T(8,128)S(1)} collective-permute-done((f32[38,8,128]{2,1,0:T(8,128)S(1)}, f32[38,8,128]{2,1,0:T(8,128)S(1)}, u32[]{:S(2)}, u32[]{:S(2)}) %collective-permute-start.12) | collective-permute-done | bytes 155680 | tf_op jit(solution)/shard_map/ppermute | solution.py:171
  72.4 2.7 %collective-permute-done.17.refs_1_ = f32[64,8,128]{2,1,0:T(8,128)S(1)} collective-permute-done((f32[64,8,128]{2,1,0:T(8,128)S(1)}, f32[64,8,128]{2,1,0:T(8,128)S(1)}, u32[]{:S(2)}, u32[]{:S(2)}) %collective-permute-start.17) | collective-permute-done | bytes 262176 | tf_op jit(solution)/shard_map/ppermute | solution.py:171
  78.1 5.0 %collective-permute-done.15.refs_1_ = f32[38,8,128]{2,1,0:T(8,128)S(1)} collective-permute-done((f32[38,8,128]{2,1,0:T(8,128)S(1)}, f32[38,8,128]{2,1,0:T(8,128)S(1)}, u32[]{:S(2)}, u32[]{:S(2)}) %collective-permute-start.15) | collective-permute-done | bytes 155680 | tf_op jit(solution)/shard_map/ppermute | solution.py:171
  85.9 1.7 %collective-permute-start.28 = (f32[128,8,128]{2,1,0:T(8,128)S(1)}, f32[128,8,128]{2,1,0:T(8,128)S(1)}, u32[]{:S(2)}, u32[]{:S(2)}) collective-permute-start(f32[128,8,128]{2,1,0:T(8,128)S(1)} %get-tuple-element.303.refs_0_), channel_id=1, source_target_pairs={{0,4},{1,3},{2,6},{3,1},{4,0},{5,7},{6,2},{7,5},{8,12},{9,11},{10,... | collective-permute-start | bytes 1572872 | tf_op jit(solution)/shard_map/ppermute | solution.py:171
  87.7 2.1 %collective-permute-start.20 = (f32[64,8,128]{2,1,0:T(8,128)S(1)}, f32[64,8,128]{2,1,0:T(8,128)S(1)}, u32[]{:S(2)}, u32[]{:S(2)}) collective-permute-start(f32[64,8,128]{2,1,0:T(8,128)S(1)} %get-tuple-element.292.refs_0_), channel_id=1, source_target_pairs={{0,8},{1,17},{2,10},{3,19},{4,12},{5,21},{6,14},{7,23},{8,0},{9,25... | collective-permute-start | bytes 786440 | tf_op jit(solution)/shard_map/ppermute | solution.py:171
  90.8 3.5 %signal_grad512.1 = (f32[1024,512]{1,0:T(8,128)}, f32[7,80]{1,0:T(8,128)}, f32[8,128]{1,0:T(8,128)S(1)}) custom-call(bf16[1024,1024]{1,0:T(8,128)(2,1)S(1)} %get-tuple-element.220.refs_6_.refs_12_.refs_0_, f8e5m2[1024,1024]{1,0:T(32,128)(4,1)S(1)} %get-tuple-element.221.refs_7_.refs_13_.refs_1_, ...), custom_call_target="tpu_custom_call", output_to_operand_aliasing={{0}: (10, {})} | custom-call | flops 14080000000 | bytes 1 | tf_op jit(solution)/shard_map/signal_grad512/pallas_call | solution.py:70
  102.5 2.0 %proj_update2.1 = (f32[512,1024]{1,0:T(8,128)}, f32[512,1024]{1,0:T(8,128)}, f32[512,1024]{1,0:T(8,128)}, bf16[512,1024]{1,0:T(8,128)(2,1)}, f32[8,128]{1,0:T(8,128)S(1)}) custom-call(f32[128,8,128]{2,1,0:T(8,128)S(1)} %get-tuple-element.303.refs_0_, f32[128,8,128]{2,1,0:T(8,128)S(1)} %collective-permute-done.30.refs_1_, f32[512,1024]{1,0:T(8,128)S(1)} %copy-done.10, ...), custom_call_target="tpu_custom_call" | custom-call | flops 6400000000 | bytes 1 | tf_op jit(solution)/shard_map/proj_update2/pallas_call | solution.py:70
  108.3 3.4 %collective-permute-done.23.refs_2_.refs_8_ = f32[152,8,128]{2,1,0:T(8,128)S(1)} collective-permute-done((f32[152,8,128]{2,1,0:T(8,128)S(1)}, f32[152,8,128]{2,1,0:T(8,128)S(1)}, u32[]{:S(2)}, u32[]{:S(2)}) %collective-permute-start.23) | collective-permute-done | bytes 622624 | tf_op jit(solution)/shard_map/ppermute | solution.py:171
  111.8 2.7 %conv_update3.1 = (f32[2,512,1024]{2,1,0:T(8,128)}, f32[2,512,1024]{2,1,0:T(8,128)}, f32[2,512,1024]{2,1,0:T(8,128)}, bf16[2,512,1024]{2,1,0:T(8,128)(2,1)}, f32[8,128]{1,0:T(8,128)S(1)}) custom-call(f32[128,8,128]{2,1,0:T(8,128)S(1)} %collective-permute-done.26.refs_0_, ...), custom_call_target="tpu_custom_call", output_to_operand_aliasing={{0}: (6, {}), {1}: (7, {}), {2}: (8, {}), {3}: (9, {})} | custom-call | flops 8640000000 | bytes 1 | tf_op jit(solution)/shard_map/conv_update3/pallas_call | solution.py:70
  116.1 3.8 %conv_update3_few.1 = (f32[2,512,1024]{2,1,0:T(8,128)}, f32[2,512,1024]{2,1,0:T(8,128)}, f32[2,512,1024]{2,1,0:T(8,128)}, bf16[2,512,1024]{2,1,0:T(8,128)(2,1)},...) custom-call(f32[128,8,128]{2,1,0:T(8,128)S(1)} %collective-permute-d, ...), custom_call_target="tpu_custom_call", output_to_operand_aliasing={{0}: (16, {}), {1}: (17, {}), {2}: (18, {}), {3}: (19, {})} | custom-call | flops 8640000000 | bytes 1 | tf_op jit(solution)/shard_map/conv_update3_few/pallas_call | solution.py:70
  (110 shorter events, 42.0 us)
Async XLA Ops:
  1.8 9.1 %collective-permute-start = (f32[72,512]{1,0:T(8,128)S(1)}, f32[72,512]{1,0:T(8,128)S(1)}, u32[]{:S(2)}, u32[]{:S(2)}) collective-permute-start(f32[72,512]{1,0:T(8,128)S(1)} %get-tuple-element.185), channel_id=1, source_target_pairs={{0,1},{1,2},{2,3},{3,4},{4,5},{5,6},{6,7},{7,8},{8,9},{9,10},{10,1... | collective-permute-start | bytes 442376 | tf_op jit(solution)/shard_map/ppermute | solution.py:410
  17.3 7.4 %collective-permute-start.1 = (f32[256,8,128]{2,1,0:T(8,128)S(1)}, f32[256,8,128]{2,1,0:T(8,128)S(1)}, u32[]{:S(2)}, u32[]{:S(2)}) collective-permute-start(f32[256,8,128]{2,1,0:T(8,128)S(1)} %get-tuple-element.227), channel_id=1, source_target_pairs={{0,1},{1,0},{2,3},{3,2},{4,5},{5,4},{6,7},{7,6},{8,9},{9,8},{10,11... | collective-permute-start | bytes 3145736 | tf_op jit(solution)/shard_map/ppermute | solution.py:171
  24.9 9.2 %collective-permute-start.5 = (f32[128,8,128]{2,1,0:T(8,128)S(1)}, f32[128,8,128]{2,1,0:T(8,128)S(1)}, u32[]{:S(2)}, u32[]{:S(2)}) collective-permute-start(f32[128,8,128]{2,1,0:T(8,128)S(1)} %get-tuple-element.242), channel_id=1, source_target_pairs={{0,4},{1,3},{2,6},{3,1},{4,0},{5,7},{6,2},{7,5},{8,12},{9,11},{10,... | collective-permute-start | bytes 1572872 | tf_op jit(solution)/shard_map/ppermute | solution.py:171
  31.1 14.0 %collective-permute-start.4 = (f32[304,8,128]{2,1,0:T(8,128)S(1)}, f32[304,8,128]{2,1,0:T(8,128)S(1)}, u32[]{:S(2)}, u32[]{:S(2)}) collective-permute-start(f32[304,8,128]{2,1,0:T(8,128)S(1)} %get-tuple-element.240), channel_id=1, source_target_pairs={{0,1},{1,0},{2,3},{3,2},{4,5},{5,4},{6,7},{7,6},{8,9},{9,8},{10,11... | collective-permute-start | bytes 3735560 | tf_op jit(solution)/shard_map/ppermute | solution.py:171
  34.2 9.2 %collective-permute-start.6 = (f32[64,8,128]{2,1,0:T(8,128)S(1)}, f32[64,8,128]{2,1,0:T(8,128)S(1)}, u32[]{:S(2)}, u32[]{:S(2)}) collective-permute-start(f32[64,8,128]{2,1,0:T(8,128)S(1)} %get-tuple-element.245), channel_id=1, source_target_pairs={{0,2},{1,5},{2,0},{3,7},{4,6},{5,1},{6,4},{7,3},{8,10},{9,13},{10,... | collective-permute-start | bytes 786440 | tf_op jit(solution)/shard_map/ppermute | solution.py:171
  35.7 12.1 %collective-permute-start.3 = (f32[128,8,128]{2,1,0:T(8,128)S(1)}, f32[128,8,128]{2,1,0:T(8,128)S(1)}, u32[]{:S(2)}, u32[]{:S(2)}) collective-permute-start(f32[128,8,128]{2,1,0:T(8,128)S(1)} %get-tuple-element.235), channel_id=1, source_target_pairs={{0,4},{1,3},{2,6},{3,1},{4,0},{5,7},{6,2},{7,5},{8,12},{9,11},{10,... | collective-permute-start | bytes 1572872 | tf_op jit(solution)/shard_map/ppermute | solution.py:171
  43.4 11.6 %collective-permute-start.8 = (f32[64,8,128]{2,1,0:T(8,128)S(1)}, f32[64,8,128]{2,1,0:T(8,128)S(1)}, u32[]{:S(2)}, u32[]{:S(2)}) collective-permute-start(f32[64,8,128]{2,1,0:T(8,128)S(1)} %get-tuple-element.256.refs_0_), channel_id=1, source_target_pairs={{0,8},{1,17},{2,10},{3,19},{4,12},{5,21},{6,14},{7,23},{8,0},{9,25... | collective-permute-start | bytes 786440 | tf_op jit(solution)/shard_map/ppermute | solution.py:171
  45.2 10.9 %collective-permute-start.7 = (f32[152,8,128]{2,1,0:T(8,128)S(1)}, f32[152,8,128]{2,1,0:T(8,128)S(1)}, u32[]{:S(2)}, u32[]{:S(2)}) collective-permute-start(f32[152,8,128]{2,1,0:T(8,128)S(1)} %get-tuple-element.255), channel_id=1, source_target_pairs={{0,4},{1,3},{2,6},{3,1},{4,0},{5,7},{6,2},{7,5},{8,12},{9,11},{10,... | collective-permute-start | bytes 1867784 | tf_op jit(solution)/shard_map/ppermute | solution.py:171
  47.9 13.4 %collective-permute-start.11 = (f32[64,8,128]{2,1,0:T(8,128)S(1)}, f32[64,8,128]{2,1,0:T(8,128)S(1)}, u32[]{:S(2)}, u32[]{:S(2)}) collective-permute-start(f32[64,8,128]{2,1,0:T(8,128)S(1)} %get-tuple-element.268), channel_id=1, source_target_pairs={{0,8},{1,17},{2,10},{3,19},{4,12},{5,21},{6,14},{7,23},{8,0},{9,25... | collective-permute-start | bytes 786440 | tf_op jit(solution)/shard_map/ppermute | solution.py:171
  55.1 13.6 %collective-permute-start.14 = (f32[64,8,128]{2,1,0:T(8,128)S(1)}, f32[64,8,128]{2,1,0:T(8,128)S(1)}, u32[]{:S(2)}, u32[]{:S(2)}) collective-permute-start(f32[64,8,128]{2,1,0:T(8,128)S(1)} %get-tuple-element.275.refs_0_), channel_id=1, source_target_pairs={{0,16},{1,9},{2,18},{3,11},{4,20},{5,13},{6,22},{7,15},{8,24},{9,1... | collective-permute-start | bytes 786440 | tf_op jit(solution)/shard_map/ppermute | solution.py:171
  56.2 7.8 %collective-permute-start.10 = (f32[76,8,128]{2,1,0:T(8,128)S(1)}, f32[76,8,128]{2,1,0:T(8,128)S(1)}, u32[]{:S(2)}, u32[]{:S(2)}) collective-permute-start(f32[76,8,128]{2,1,0:T(8,128)S(1)} %get-tuple-element.266), channel_id=1, source_target_pairs={{0,2},{1,5},{2,0},{3,7},{4,6},{5,1},{6,4},{7,3},{8,10},{9,13},{10,... | collective-permute-start | bytes 933896 | tf_op jit(solution)/shard_map/ppermute | solution.py:171
  61.3 8.0 %collective-permute-start.13 = (f32[32,8,128]{2,1,0:T(8,128)S(1)}, f32[32,8,128]{2,1,0:T(8,128)S(1)}, u32[]{:S(2)}, u32[]{:S(2)}) collective-permute-start(f32[32,8,128]{2,1,0:T(8,128)S(1)} %get-tuple-element.274), channel_id=1, source_target_pairs={{0,2},{1,5},{2,0},{3,7},{4,6},{5,1},{6,4},{7,3},{8,10},{9,13},{10,... | collective-permute-start | bytes 393224 | tf_op jit(solution)/shard_map/ppermute | solution.py:171
  64.0 8.0 %collective-permute-start.12 = (f32[38,8,128]{2,1,0:T(8,128)S(1)}, f32[38,8,128]{2,1,0:T(8,128)S(1)}, u32[]{:S(2)}, u32[]{:S(2)}) collective-permute-start(f32[38,8,128]{2,1,0:T(8,128)S(1)} %get-tuple-element.272), channel_id=1, source_target_pairs={{0,8},{1,17},{2,10},{3,19},{4,12},{5,21},{6,14},{7,23},{8,0},{9,25... | collective-permute-start | bytes 466952 | tf_op jit(solution)/shard_map/ppermute | solution.py:171
  72.0 11.1 %collective-permute-start.15 = (f32[38,8,128]{2,1,0:T(8,128)S(1)}, f32[38,8,128]{2,1,0:T(8,128)S(1)}, u32[]{:S(2)}, u32[]{:S(2)}) collective-permute-start(f32[38,8,128]{2,1,0:T(8,128)S(1)} %get-tuple-element.279.refs_0_), channel_id=1, source_target_pairs={{0,16},{1,9},{2,18},{3,11},{4,20},{5,13},{6,22},{7,15},{8,24},{9,1... | collective-permute-start | bytes 466952 | tf_op jit(solution)/shard_map/ppermute | solution.py:171
  76.7 10.9 %collective-permute-start.19 = (f32[32,8,128]{2,1,0:T(8,128)S(1)}, f32[32,8,128]{2,1,0:T(8,128)S(1)}, u32[]{:S(2)}, u32[]{:S(2)}) collective-permute-start(f32[32,8,128]{2,1,0:T(8,128)S(1)} %get-tuple-element.286.refs_0_), channel_id=1, source_target_pairs={{0,2},{1,5},{2,0},{3,7},{4,6},{5,1},{6,4},{7,3},{8,10},{9,13},{10,... | collective-permute-start | bytes 393224 | tf_op jit(solution)/shard_map/ppermute | solution.py:171
  83.2 7.6 %collective-permute-start.9 = (f32[72,512]{1,0:T(8,128)S(1)}, f32[72,512]{1,0:T(8,128)S(1)}, u32[]{:S(2)}, u32[]{:S(2)}) collective-permute-start(f32[72,512]{1,0:T(8,128)S(1)} %get-tuple-element.262), channel_id=1, source_target_pairs={{1,0},{2,1},{3,2},{4,3},{5,4},{6,5},{7,6},{8,7},{9,8},{10,9},{11,1... | collective-permute-start | bytes 442376 | tf_op jit(solution)/shard_map/ppermute | solution.py:549
  84.7 15.7 %collective-permute-start.30 = (f32[128,8,128]{2,1,0:T(8,128)S(1)}, f32[128,8,128]{2,1,0:T(8,128)S(1)}, u32[]{:S(2)}, u32[]{:S(2)}) collective-permute-start(f32[128,8,128]{2,1,0:T(8,128)S(1)} %get-tuple-element.303.refs_0_), channel_id=1, source_target_pairs={{0,1},{1,0},{2,3},{3,2},{4,5},{5,4},{6,7},{7,6},{8,9},{9,8},{10,11... | collective-permute-start | bytes 1572872 | tf_op jit(solution)/shard_map/ppermute | solution.py:171
  85.9 15.9 %collective-permute-start.28 = (f32[128,8,128]{2,1,0:T(8,128)S(1)}, f32[128,8,128]{2,1,0:T(8,128)S(1)}, u32[]{:S(2)}, u32[]{:S(2)}) collective-permute-start(f32[128,8,128]{2,1,0:T(8,128)S(1)} %get-tuple-element.303.refs_0_), channel_id=1, source_target_pairs={{0,4},{1,3},{2,6},{3,1},{4,0},{5,7},{6,2},{7,5},{8,12},{9,11},{10,... | collective-permute-start | bytes 1572872 | tf_op jit(solution)/shard_map/ppermute | solution.py:171
  87.7 8.0 %collective-permute-start.20 = (f32[64,8,128]{2,1,0:T(8,128)S(1)}, f32[64,8,128]{2,1,0:T(8,128)S(1)}, u32[]{:S(2)}, u32[]{:S(2)}) collective-permute-start(f32[64,8,128]{2,1,0:T(8,128)S(1)} %get-tuple-element.292.refs_0_), channel_id=1, source_target_pairs={{0,8},{1,17},{2,10},{3,19},{4,12},{5,21},{6,14},{7,23},{8,0},{9,25... | collective-permute-start | bytes 786440 | tf_op jit(solution)/shard_map/ppermute | solution.py:171
  89.8 8.8 %collective-permute-start.22 = (f32[76,8,128]{2,1,0:T(8,128)S(1)}, f32[76,8,128]{2,1,0:T(8,128)S(1)}, u32[]{:S(2)}, u32[]{:S(2)}) collective-permute-start(f32[76,8,128]{2,1,0:T(8,128)S(1)} %get-tuple-element.295.refs_0_), channel_id=1, source_target_pairs={{0,2},{1,5},{2,0},{3,7},{4,6},{5,1},{6,4},{7,3},{8,10},{9,13},{10,... | collective-permute-start | bytes 933896 | tf_op jit(solution)/shard_map/ppermute | solution.py:171
  95.8 9.2 %collective-permute-start.26 = (f32[128,8,128]{2,1,0:T(8,128)S(1)}, f32[128,8,128]{2,1,0:T(8,128)S(1)}, u32[]{:S(2)}, u32[]{:S(2)}) collective-permute-start(f32[128,8,128]{2,1,0:T(8,128)S(1)} %get-tuple-element.294.refs_0_), channel_id=1, source_target_pairs={{0,4},{1,3},{2,6},{3,1},{4,0},{5,7},{6,2},{7,5},{8,12},{9,11},{10,... | collective-permute-start | bytes 1572872 | tf_op jit(solution)/shard_map/ppermute | solution.py:171
  97.4 18.6 %collective-permute-start.21 = (f32[128,8,128]{2,1,0:T(8,128)S(1)}, f32[128,8,128]{2,1,0:T(8,128)S(1)}, u32[]{:S(2)}, u32[]{:S(2)}) collective-permute-start(f32[128,8,128]{2,1,0:T(8,128)S(1)} %get-tuple-element.294.refs_0_), channel_id=1, source_target_pairs={{0,1},{1,0},{2,3},{3,2},{4,5},{5,4},{6,7},{7,6},{8,9},{9,8},{10,11... | collective-permute-start | bytes 1572872 | tf_op jit(solution)/shard_map/ppermute | solution.py:171
  98.7 15.8 %collective-permute-start.25 = (f32[152,8,128]{2,1,0:T(8,128)S(1)}, f32[152,8,128]{2,1,0:T(8,128)S(1)}, u32[]{:S(2)}, u32[]{:S(2)}) collective-permute-start(f32[152,8,128]{2,1,0:T(8,128)S(1)} %get-tuple-element.297.refs_1_.refs_6_), channel_id=1, source_target_pairs={{0,1},{1,0},{2,3},{3,2},{4,5},{5,4},{6,7},{7,6},{8,9},{9,8},{10,11... | collective-permute-start | bytes 1867784 | tf_op jit(solution)/shard_map/ppermute | solution.py:171
  100.4 11.3 %collective-permute-start.23 = (f32[152,8,128]{2,1,0:T(8,128)S(1)}, f32[152,8,128]{2,1,0:T(8,128)S(1)}, u32[]{:S(2)}, u32[]{:S(2)}) collective-permute-start(f32[152,8,128]{2,1,0:T(8,128)S(1)} %get-tuple-element.297.refs_1_.refs_6_), channel_id=1, source_target_pairs={{0,4},{1,3},{2,6},{3,1},{4,0},{5,7},{6,2},{7,5},{8,12},{9,11},{10,... | collective-permute-start | bytes 1867784 | tf_op jit(solution)/shard_map/ppermute | solution.py:171
  (23 other events, 98.3 us)
where the time goes:
time: 120 us
  Pallas kernels  52.2 us (44%)
  starting transfers between devices  36.8 us (31%)
  waiting for transfers between devices  29.5 us (25%)
  between operations  1.36 us (1%)
    pallas_call x40, Pallas kernels, call(): pl.pallas_call(run, out_shape=[kinds[id(s)](*o) for o, s in zip(outs, out...  52.2 us
    ppermute x29, starting transfers between devices, swap(): return lax.ppermute(x, axes, self.pairs[step])  32.7 us
    ppermute x29, waiting for transfers between devices, swap(): return lax.ppermute(x, axes, self.pairs[step])  29.5 us
    ppermute x1, starting transfers between devices, solve(): halo = lax.ppermute(packed, axes, [(i, i + 1) for i in range(count - 1)])  2.63 us
  transfers between devices with their start and end apart: 31, of which 13 were waited for; matrix products, arithmetic and copies ran while one was open for 0% of the time, Pallas kernels for 34%

commit v1 on v0

--- a/solution.py
+++ b/solution.py
@@ -28,16 +28,18 @@
 
 TOKEN = ((8, 128), f32)
 
-RATE = 3.2e9
+RATE = 2.9e9
 TIMES = {
-    "pack": 1, "late_gates": 8, "early_gates": 6, "proj_grad_send": 1.8, "gate_grad": 5.8,
-    "tap0_send": 1.8, "tap0_keep_tap1_send": 4.5, "tap1_keep": 1.8, "mix": 2.8, "signal_grad": 4.4,
-    "back": 1.4, "update1_few": 2, "update1": 1.4, "update2": 2, "update3": 2.7, "update4": 3.3,
+    "pack": 1, "late_gates": 4, "early_gates": 4.4, "gate_grad": 3.4, "proj_grad": 1.4, "tap0_grad": 1.4,
+    "tap1_grad0": 2, "tap1_grad1": 1.4,
 }
-FOLD = 0.1
+WORK = {"do": 0.7, "mix": 1.5, "sg": 2.8, "back": 0.5, "few": 0.8, "u1": 0.7, "u2": 1.3, "u3": 1.9, "u4": 2.5}
+FOLD = 0.03
 
 
 def expected(name):
+    if name.startswith("do_"):
+        return sum(WORK.get(word, 3) for word in name.split("_"))
     for key in sorted(TIMES, key=len, reverse=True):
         if key in name:
             return TIMES[key]
@@ -95,6 +97,44 @@
     return high, (x - high.astype(f32)).astype(bf16)
 
 
+class Part:
+    def __init__(self, name, ins, outs, start, done, old=(), scratch=(), to_hbm=True):
+        self.name, self.ins, self.outs, self.start, self.done = name, list(ins), list(outs), start, done
+        self.old, self.scratch, self.to_hbm = list(old), list(scratch), to_hbm
+
+
+def run_parts(order, parts):
+    ins, specs, outs, out_specs, scratch, aliases = [], [], [], [], [], {}
+    for part in parts:
+        for i in range(len(part.old)):
+            aliases[len(ins) + len(part.ins) + i] = len(outs) + i
+        ins += part.ins + part.old
+        specs += [VMEM] * len(part.ins) + [HBM] * len(part.old)
+        outs += part.outs
+        out_specs += [HBM if part.to_hbm else VMEM] * len(part.outs)
+        scratch += part.scratch
+    n_in, n_out = len(ins), len(outs)
+
+    def body(*refs):
+        ins, outs, scratch = list(refs[:n_in]), list(refs[n_in : n_in + n_out]), list(refs[n_in + n_out :])
+        copies = []
+        for part in parts:
+            mine = [ins.pop(0) for _ in part.ins]
+            del ins[: len(part.old)]
+            mine += [outs.pop(0) for _ in part.outs]
+            mine += [scratch.pop(0) for _ in part.scratch]
+            copies += part.start(*mine)
+        for copy in copies:
+            copy.wait()
+
+    name = "_".join(["do"] + [part.name for part in parts])
+    result = order.call(
+        body, name, ins, outs, specs=specs, out_specs=out_specs, scratch=scratch, aliases=aliases, limit=20
+    )
+    for part in parts:
+        part.done([result.pop(0) for _ in part.outs])
+
+
 def put(refs, where, x, scale):
     high = x.astype(bf16)
     refs[0][where] = high
@@ -300,12 +340,8 @@
 
 def late_body(rows, *refs):
     signal, conv, cond, mel, slots, starts, bias = refs[:7]
-    far, near, (table, frames, sem) = refs[7:10], refs[28:31], refs[31:]
-    x0, x1, d, w = (refs[i : i + 3] for i in (10, 13, 16, 19))
-    sel, g, ca, cb = refs[22], refs[23:26], refs[26], refs[27]
-    copies = [pltpu.make_async_copy(a, b, sem.at[i]) for i, (a, b) in enumerate(zip(far, near))]
-    for copy in copies:
-        copy.start()
+    x0, x1, d, w = (refs[i : i + 3] for i in (7, 10, 13, 16))
+    sel, g, ca, cb, table, frames = refs[19], refs[20:23], *refs[23:]
     first = HALF - DILATION
     picks(slots, 1, mel.shape[0], sel)
     frame_terms(mel, None, cond, bias, table, frames)
@@ -322,8 +358,6 @@
             products.append(preact_block(d, x1, sel, w, table, cols))
         gates(*products, blocks[0], g, ca, cb)
     put(x0, slice(None), signal[0:HALF, :], SIGNAL_SCALE)
-    for copy in copies:
-        copy.wait()
 
 
 def early_body(rows, *refs):
@@ -338,24 +372,25 @@
     put(d, slice(0, DILATION), halo[0:DILATION, :] * usable[0:DILATION], SIGNAL_SCALE)
     rest = HALF - DILATION
     put(d, slice(DILATION, None), signal[0:rest, :] * usable[DILATION:], SIGNAL_SCALE)
-    usum[...] = jnp.zeros((8, 2 * RESID), f32)
+    totals = [jnp.zeros((8, RESID), f32), jnp.zeros((8, RESID), f32)]
 
     def part_cotangents(first, count):
-        for r in range(first, first + count, 128):
+        for r in range(first, first + count, 32):
             for k, part in enumerate((resid_cotan, skip_cotan)):
-                span = slice(k * RESID, (k + 1) * RESID)
-                value = part[r : r + 128, :]
-                put(u, (slice(r, r + 128), span), value, UP_SCALE)
-                usum[:, span] += jnp.sum(value.reshape(16, 8, RESID), 0)
-
+                value = part[r : r + 32, :]
+                put(u, (slice(r, r + 32), slice(k * RESID, (k + 1) * RESID)), value, UP_SCALE)
+                totals[k] = totals[k] + jnp.sum(value.reshape(4, 8, RESID), 0)
+
+    for r in range(0, HALF, 32):
+        put(p, slice(r, r + 32), proj[r : r + 32, :], PROJ_SCALE)
     for j in range(HALF // BLOCK):
         tc, sc = (slice(c + j * BLOCK, c + (j + 1) * BLOCK) for c in (0, HALF))
+        part_cotangents(j * rows // 2, rows // 4)
         tanh_in = preact_block(d, x, sel, w, table, tc)
-        part_cotangents(j * rows // 2, rows // 4)
+        part_cotangents(j * rows // 2 + rows // 4, rows // 4)
         sigm_in = preact_block(d, x, sel, w, table, sc)
-        part_cotangents(j * rows // 2 + rows // 4, rows // 4)
         gates(tanh_in, sigm_in, tc, g, ca, cb)
-    put(p, slice(None), proj[...], PROJ_SCALE)
+    usum[...] = jnp.concatenate(totals, 1)
 
 
 def put_tiles(out, value, col0, stride=None):
@@ -416,19 +451,17 @@
     square = [((GATE, GATE), t) for t in wide]
     pick = ((HALF, 128), bf16)
     small_scratch = [pltpu.VMEM((128, GATE), bf16), pltpu.VMEM((16, 128), f32)]
-    held = [resid_cotan, skip_cotan, proj_weight]
     out = call(
         lambda *r: late_body(rows, *r), "late_gates",
-        [signal, conv_weight, cond_weight, mel_frames, slots, starts, bias, *held],
-        [*half, *half, *half, *square, pick, *half_gate, half32, half32, *((x.shape, x.dtype) for x in held)],
-        specs=[VMEM] * 7 + [HBM] * 3,
-        scratch=[*small_scratch, pltpu.SemaphoreType.DMA((3,))],
+        [signal, conv_weight, cond_weight, mel_frames, slots, starts, bias],
+        [*half, *half, *half, *square, pick, *half_gate, half32, half32], scratch=small_scratch,
     )
     x0, x1, d1, w = (out[i : i + 3] for i in (0, 3, 6, 9))
-    sel1, g1, ca1, cb1, (resid_in, skip_in, proj_in) = out[12], out[13:16], out[16], out[17], out[18:]
+    sel1, g1, ca1, cb1 = out[12], out[13:16], out[16], out[17]
     out = call(
         lambda *r: early_body(rows, *r), "early_gates",
-        [halo, signal, *x0, *w, cond_weight, mel_frames, slots, starts, bias, resid_in, skip_in, proj_in],
+        [halo, signal, *x0, *w, cond_weight, mel_frames, slots, starts, bias,
+         resid_cotan, skip_cotan, proj_weight],
         [*half, pick, *half_gate, half32, half32, *(((GATE, GATE), t) for t in fine),
          *(((HALF, GATE), t) for t in fine), ((8, GATE), f32)],
         scratch=small_scratch,
@@ -437,62 +470,39 @@
     u, p, usum = out[9:12], out[12:15], out[15]
 
     tiles = ((2 * QUARTER, 8, 128), f32)
-
-    def proj_half(own):
-        def body(*refs):
-            weight_grad(refs[:6], half_cols(own), refs[6:9], refs[9], GATED_SCALE * UP_SCALE)
-
-        return body
-
-    gated = [*g0, *g1, *u]
-    (proj_send,) = call(proj_half(False), "proj_grad_send", gated, [tiles])
-    proj_sum = Sum(order, pairs, "proj", proj_send, WHOLE[0])
-
-    def gate_grad(*refs):
-        u, p, (ca0, ca1, cb0, cb1) = refs[6:9], refs[9:12], refs[12:16]
-        out, gp = refs[16], refs[17:20]
-        proj_half(True)(*refs[:9], out)
-        right = [x[...] for x in p]
-        for r in range(0, rows, BLOCK):
-            span = slice(r, r + BLOCK)
-            grad = product([x[span, :] for x in u], right, NT, UP_SCALE * PROJ_SCALE)
-            ca, cb = (ca0, cb0) if r < HALF else (ca1, cb1)
-            inner = slice(r % HALF, r % HALF + BLOCK)
-            put(gp, (span, slice(0, HALF)), grad * ca[inner, :], GRAD_SCALE)
-            put(gp, (span, slice(HALF, GATE)), grad * cb[inner, :], GRAD_SCALE)
-
-    proj_sum.rest, *gp = call(
-        gate_grad, "gate_grad", [*gated, *p, ca0, ca1, cb0, cb1], [tiles, *square]
-    )
-    proj_sum.advance()
-
-    def tap_half(own, stride=None):
-        def body(*refs):
-            weight_grad(
-                refs[:6], half_cols(own), refs[6:9], refs[9], SIGNAL_SCALE * GRAD_SCALE, stride
-            )
-
-        return body
-
-    (send,) = call(tap_half(False), "tap0_send", [*d0, *d1, *gp], [tiles])
-    tap0_sum = Sum(order, Pairs("tap0"), "tap0", send, WHOLE[1])
-
     few = 24
     while (QUARTER + few) % max(1, count // 4):
         few += 8
     quarter = QUARTER + few
     wide_tiles = ((2 * quarter, 8, 128), f32)
+    state = {}
+    sums = {}
+
+    def grad_half(own, scale, stride=None):
+        def body(*refs):
+            weight_grad(refs[:6], half_cols(own), refs[6:9], refs[9], scale, stride)
+
+        return body
+
+    def proj_grad(own):
+        body = grad_half(own, GATED_SCALE * UP_SCALE)
+        (out,) = call(body, f"proj_grad{own:d}", [*g0, *g1, *u], [tiles])
+        return out
+
+    def tap0_grad(own):
+        body = grad_half(own, SIGNAL_SCALE * GRAD_SCALE)
+        (out,) = call(body, f"tap0_grad{own:d}", [*d0, *d1, *state["gp"]], [tiles])
+        return out
 
     def tap1_half(own, *refs):
         both, out = refs[9:]
-        tap_half(own, quarter)(*refs[:9], out)
+        grad_half(own, SIGNAL_SCALE * GRAD_SCALE, quarter)(*refs[:9], out)
         for q in range(2):
             out[pl.ds(q * quarter + QUARTER, few)] = both[core_half(own) * 2 + q]
 
-    def tap0_keep_tap1_send(*refs):
-        d, x, gp, (sel0, sel1, usum, mel, halo) = refs[:6], refs[6:12], refs[12:15], refs[15:20]
-        zero_keep, one_send, both, frame_grad, frames = refs[20:]
-        tap_half(True)(*d, *gp, zero_keep)
+    def tap1_first(*refs):
+        x, gp, (sel0, sel1, usum, mel, halo) = refs[:6], refs[6:9], refs[9:14]
+        out, both, frame_grad, frames = refs[14:]
         sel = jnp.concatenate([sel0[:, 0:16], sel1[:, 0:16]], 0)
         found = dot(sel, gp[0][...], TN)
         found += dot(sel.astype(wide8), gp[2][...], TN) * (1.0 / (LOW * GRAD_SCALE))
@@ -510,19 +520,45 @@
             lane = slice(128 * i, 128 * i + 128)
             both[3, 8, i : i + 1, :] = found[15:16, lane]
             both[3, 9, i : i + 1, :] = sums[:, lane]
-        tap1_half(False, *x, *gp, both, one_send)
-
-    tap0_sum.rest, send, few_grad, frame_grad = call(
-        tap0_keep_tap1_send, "tap0_keep_tap1_send",
-        [*d0, *d1, *x0, *x1, *gp, sel0, sel1, usum, mel_frames, halo],
-        [tiles, wide_tiles, ((4, few, 8, 128), f32), ((16, GATE), f32)],
-        scratch=[pltpu.VMEM((16, 128), f32)],
-    )
-    tap1_sum = Sum(order, Pairs("tap1"), "tap1", send, WHOLE[2])
-    tap0_sum.advance()
-    (tap1_sum.rest,) = call(
-        lambda *r: tap1_half(True, *r), "tap1_keep", [*x0, *x1, *gp, few_grad], [wide_tiles]
-    )
+        tap1_half(False, *x, *gp, both, out)
+
+    def tap1_grad(own):
+        ins = [*x0, *x1, *state["gp"]]
+        if own:
+            (out,) = call(
+                lambda *r: tap1_half(True, *r), "tap1_grad1", [*ins, state["few_grad"]], [wide_tiles]
+            )
+            return out
+        out, state["few_grad"], state["frame_grad"] = call(
+            tap1_first, "tap1_grad0", [*ins, sel0, sel1, usum, mel_frames, halo],
+            [wide_tiles, ((4, few, 8, 128), f32), ((16, GATE), f32)],
+            scratch=[pltpu.VMEM((16, 128), f32)],
+        )
+        return out
+
+    def gate_grad():
+        def body(*refs):
+            u, p, (ca0, ca1, cb0, cb1), gp = refs[:3], refs[3:6], refs[6:10], refs[10:]
+            right = [x[...] for x in p]
+            for r in range(0, rows, BLOCK):
+                span = slice(r, r + BLOCK)
+                grad = product([x[span, :] for x in u], right, NT, UP_SCALE * PROJ_SCALE)
+                ca, cb = (ca0, cb0) if r < HALF else (ca1, cb1)
+                inner = slice(r % HALF, r % HALF + BLOCK)
+                put(gp, (span, slice(0, HALF)), grad * ca[inner, :], GRAD_SCALE)
+                put(gp, (span, slice(HALF, GATE)), grad * cb[inner, :], GRAD_SCALE)
+
+        state["gp"] = call(body, "gate_grad", [*u, *p, ca0, ca1, cb0, cb1], square)
+
+    grads = {"P": ("proj", proj_grad), "0": ("tap0", tap0_grad), "1": ("tap1", tap1_grad)}
+
+    def first_half(key):
+        name, grad = grads[key]
+        whole = WHOLE["P01".index(key)]
+        sums[key] = Sum(order, Pairs(name), name, grad(False), whole)
+
+    def second_half(key):
+        sums[key].rest = grads[key][1](True)
 
     def tap_back(gp, w, rows_, tap):
         span = slice(tap * RESID, (tap + 1) * RESID)
@@ -538,20 +574,22 @@
         out[DILATION:, :] = jnp.zeros((8, RESID), f32)
         out[DILATION : DILATION + slot_count, :MELS] = mels[:slot_count]
         own[...] = mels[slot_count : 2 * slot_count]
-
-    state = {}
+        return []
 
     def back():
-        state["back"], state["mel_own"] = call(
-            back_body, "back", [*gp, *w, frame_grad, cond_weight, starts],
-            [((DILATION + 8, RESID), f32), ((slot_count, MELS), f32)],
+        def done(result):
+            state["mel_own"] = result[1]
+            state["came"] = lax.ppermute(result[0], axes, [(i, i - 1) for i in range(1, count)])
+
+        return Part(
+            "back", [*state["gp"], *w, state["frame_grad"], cond_weight, starts],
+            [((DILATION + 8, RESID), f32), ((slot_count, MELS), f32)], back_body, done, to_hbm=False,
         )
-        state["came"] = lax.ppermute(state["back"], axes, [(i, i - 1) for i in range(1, count)])
 
     def mix(r):
-        def body(*refs):
+        def start(*refs):
             g, p, (bias, signal) = refs[:3], refs[3:6], refs[6:8]
-            outs, (held, sem) = refs[-4:-2], refs[-2:]
+            outs, (held, sem) = refs[8:10], refs[10:]
             copies = []
             for s in range(0, HALF, BLOCK):
                 inner = slice(s, s + BLOCK)
@@ -571,31 +609,28 @@
                         )
                     )
                     copies[-1].start()
-            for copy in copies:
-                copy.wait()
-
-        old = state.get("mixed", [])
-        state["mixed"] = call(
-            body, f"mix{r}", [*(g0 if r < HALF else g1), *p, bias, signal, *old],
-            [((rows, RESID), f32)] * 2, aliases={8 + i: i for i in range(len(old))},
-            specs=[VMEM] * 8 + [HBM] * len(old), out_specs=[HBM] * 2,
+            return copies
+
+        return Part(
+            "mix", [*(g0 if r < HALF else g1), *p, bias, signal], [((rows, RESID), f32)] * 2,
+            start, lambda result: state.update(mixed=result), old=state.get("mixed", ()),
             scratch=[pltpu.VMEM((2, HALF, RESID), f32), pltpu.SemaphoreType.DMA((4,))],
         )
 
     def signal_grad(r):
         last = r + HALF == rows
 
-        def body(*refs):
+        def start(*refs):
             gp, w, (starts, resid_cotan) = refs[:3], refs[3:6], refs[6:8]
             held, mels, sem = refs[-3:]
             copies = []
             if last:
-                came, own, _, out, mel_grad = refs[8:-3]
+                came, own, out, mel_grad = refs[8:-3]
                 mels[...] = own[...] + came[DILATION : DILATION + slot_count, :MELS]
                 copies.append(pltpu.make_async_copy(mels, mel_grad, sem.at[2]))
                 copies[0].start()
             else:
-                out = refs[-4]
+                out = refs[8]
             usable = columns(usable_row(starts, 0, rows, rows), rows)
             for s in range(r, r + HALF, BLOCK):
                 span = slice(s, s + BLOCK)
@@ -612,18 +647,16 @@
                     )
                 )
                 copies[-1].start()
-            for copy in copies:
-                copy.wait()
-
-        ins = [*gp, *w, starts, resid_in]
+            return copies
+
+        ins = [*state["gp"], *w, starts, resid_cotan]
         outs = [((rows, RESID), f32)]
         if last:
             ins += [state["came"], state["mel_own"]]
             outs += [((slot_count, MELS), f32)]
-        old = state.get("signal_grad", [])
-        state["signal_grad"] = call(
-            body, f"signal_grad{r}", ins + list(old), outs, aliases={len(ins): 0} if old else {},
-            specs=[VMEM] * len(ins) + [HBM] * len(old), out_specs=[HBM] * len(outs),
+        return Part(
+            "sg", ins, outs, start, lambda result: state.update(signal_grad=result),
+            old=state.get("signal_grad", ()),
             scratch=[pltpu.VMEM((HALF, RESID), f32), pltpu.VMEM((slot_count, MELS), f32),
                      pltpu.SemaphoreType.DMA((3,))],
         )
@@ -651,7 +684,7 @@
 
     def update_few(pieces, ins, outs, held, grads, sem):
         for k, piece in enumerate(pieces):
-            first = tap1_sum.pairs.quarter(k) * 24
+            first = sums["1"].pairs.quarter(k) * 24
             grads[pl.ds(first, 24)] = piece[QUARTER : QUARTER + 24]
         for r in range(0, MELS, 16):
             span = slice(r, r + 16)
@@ -675,28 +708,14 @@
             copy.start()
         return copies
 
-    def update(key, items, few_too=False):
+    def update(key, items):
         trio, rate = matrices[key]
-        old = state.get(key, [])
         n = len(items)
-        ins = [total.pieces[k] for total, k, _ in items] + [*trio]
-        if few_too:
-            ins += [*tap1_sum.pieces, *few_args]
-
-        def body(*refs):
-            refs = list(refs)
-            take = lambda count: [refs.pop(0) for _ in range(count)]
-            gs, trio_refs = take(n), take(3)
-            few_refs = take(10) if few_too else []
-            take(len(old))
-            outs = take(4)
-            few_outs = take(8) if few_too else []
-            held, sem = take(4), refs.pop(0)
+
+        def start(*refs):
+            gs, trio_refs, outs = refs[:n], refs[n : n + 3], refs[n + 3 : n + 7]
+            held, sem = refs[n + 7 : n + 11], refs[n + 11]
             copies = []
-            if few_too:
-                copies += update_few(
-                    few_refs[:4], few_refs[4:], few_outs, refs[:8], refs[8], refs[9]
-                )
             for i, (total, k, lead) in enumerate(items):
                 first = pl.multiple_of(total.pairs.quarter(k) * QUARTER, QUARTER)
                 parts = [x if lead is None else x.at[lead] for x in (*trio_refs, *outs)]
@@ -720,56 +739,67 @@
                         )
                     )
                     copies[-1].start()
-            for copy in copies:
-                copy.wait()
-
-        scratch = [pltpu.VMEM((n * QUARTER, GATE), t) for t in kinds]
-        scratch += [pltpu.SemaphoreType.DMA((4 * n,))]
-        if few_too:
-            scratch += [pltpu.VMEM(*x) for x in few_shapes]
-            scratch += [pltpu.VMEM((96, 8, 128), f32), pltpu.SemaphoreType.DMA((8,))]
-        result = call(
-            body, f"{key}_update{n}" + ("_few" if few_too else ""), [*ins, *old],
-            [(trio[0].shape, t) for t in kinds] + (few_shapes if few_too else []),
-            specs=[VMEM] * len(ins) + [HBM] * len(old),
-            out_specs=[HBM] * (12 if few_too else 4), scratch=scratch,
-            aliases={len(ins) + i: i for i in range(len(old))},
+            return copies
+
+        return Part(
+            f"u{n}", [total.pieces[k] for total, k, _ in items] + [*trio],
+            [(trio[0].shape, t) for t in kinds], start,
+            lambda result: state.update({key: result}), old=state.get(key, ()),
+            scratch=[pltpu.VMEM((n * QUARTER, GATE), t) for t in kinds]
+            + [pltpu.SemaphoreType.DMA((4 * n,))],
         )
-        state[key] = result[:4]
-        if few_too:
-            state["few"] = result[4:]
-
-    def spread(total):
+
+    def few_update():
+        def start(*refs):
+            return update_few(refs[:4], refs[4:10], refs[10:18], refs[18:26], refs[26], refs[27])
+
+        return Part(
+            "few", [*sums["1"].pieces, *few_args], few_shapes, start,
+            lambda result: state.update(few=result),
+            scratch=[pltpu.VMEM(*x) for x in few_shapes]
+            + [pltpu.VMEM((96, 8, 128), f32), pltpu.SemaphoreType.DMA((8,))],
+        )
+
+    def spread(key):
+        total = sums[key]
         while not total.done:
             total.advance()
         total.pieces = [total.piece, total.pairs.swap(total.piece, 0), total.pairs.swap(total.piece, 1)]
 
-    def relay(total):
+    def relay(key):
+        total = sums[key]
         total.pieces.append(total.pairs.swap(total.pieces[2], 0))
 
-    trees = {"P": (proj_sum, "proj", None), "0": (tap0_sum, "conv", 0), "1": (tap1_sum, "conv", 1)}
+    owners = {"P": ("proj", None), "0": ("conv", 0), "1": ("conv", 1)}
     fill = {"back": back}
     for i in range(2):
         fill[f"mix{i}"] = lambda i=i: mix(i * HALF)
         fill[f"sg{i}"] = lambda i=i: signal_grad(i * HALF)
+
+    def updates(word):
+        named = {}
+        for letter in word[1:]:
+            if letter in owners:
+                key, lead = owners[letter]
+                total = sums[letter]
+            elif letter in "abcd":
+                named.setdefault(key, []).append((total, "abcd".index(letter), lead))
+        return [update(key, items) for key, items in named.items()] + (
+            [few_update()] if "f" in word else []
+        )
+
     for word in SCRIPT.split():
-        if word in trees:
-            trees[word][0].advance()
-        elif word in fill:
-            fill[word]()
-        elif word[0] == "s":
-            spread(trees[word[1]][0])
-        elif word[0] == "r":
-            relay(trees[word[1]][0])
+        if word in owners:
+            sums[word].advance()
+        elif word == "gg":
+            gate_grad()
+        elif len(word) == 2 and word[0] in "jksr":
+            {"j": first_half, "k": second_half, "s": spread, "r": relay}[word[0]](word[1])
         else:
-            items, name = [], None
-            for letter in word[1:]:
-                if letter in trees:
-                    name = letter
-                elif letter in "abcd":
-                    total, key, lead = trees[name]
-                    items.append((total, "abcd".index(letter), lead))
-            update(key, items, "f" in word)
+            work = []
+            for item in word.split("+"):
+                work += updates(item) if item[0] == "=" else [fill[item]()]
+            run_parts(order, work)
     proj_new, conv_new = state["proj"], state["conv"]
     cond_new, bias_new = state["few"][:4], [x.reshape(-1) for x in state["few"][4:]]
     result = [*state["mixed"], *state["signal_grad"]]
@@ -780,7 +810,8 @@
 
 WHOLE = (2, 1, 1)
 SCRIPT = """
-P sg0 P 1 back 0 mix0 P 1 mix1 0 1 P 0 1 P 0 1 0 sP rP 1 sg1 0 s0 1 s1 =0a =Pab r0 =Pd =Pc r1 =0cd1c =1b =0b1adf
+jP gg kP P j0 k0 j1 k1 P 0 sg0 P 1 back 0 mix0 P 1 mix1 0 1 P 0 1 0 P 1 0 sP rP sg1 1 0 s0 =Pab 1 s1 r0 =Pd0a
+r1 =0cd1bc =0b1adPcf
 """
 
 

time: 120 us -> 114 us (0.950); the launches traced: 120 us -> 112 us
  Pallas kernels: 52.2 us -> 47 us
  starting transfers between devices: 36.8 us -> 35.1 us
    pallas_call x40 -> x39, Pallas kernels: 52.2 us -> 47 us  [call(): pl.pallas_call(run, out_shape=[kinds[id(s)](*o) for o, s in zip(outs, out...]
    ppermute x29, starting transfers between devices: 32.7 us -> 31 us  [swap(): return lax.ppermute(x, axes, self.pairs[step])]
  transfers between devices with their start and end apart: 31 -> 31, of which waited for: 13 -> 13; matrix products, arithmetic and copies ran while one was open for 0% -> 0% of each run, Pallas kernels for 34% -> 32%
where the time goes in v1:
time: 114 us; the launch traced here: 112 us
  Pallas kernels  47 us (41%)
  starting transfers between devices  35.1 us (31%)
  waiting for transfers between devices  28.8 us (25%)
  between operations  1.43 us (1%)
    pallas_call x39, Pallas kernels, call(): pl.pallas_call(run, out_shape=[kinds[id(s)](*o) for o, s in zip(outs, out...  47 us
    ppermute x29, starting transfers between devices, swap(): return lax.ppermute(x, axes, self.pairs[step])  31 us
    ppermute x29, waiting for transfers between devices, swap(): return lax.ppermute(x, axes, self.pairs[step])  28.8 us
    ppermute x1, starting transfers between devices, solve(): halo = lax.ppermute(packed, axes, [(i, i + 1) for i in range(count - 1)])  2.63 us
  transfers between devices with their start and end apart: 31, of which 13 were waited for; matrix products, arithmetic and copies ran while one was open for 0% of the time, Pallas kernels for 32%

profile of v1, /device:TPU:0, one launch (start us, length us, event | category | flops | bytes accessed | tf_op | source)
XLA Modules:
  0.0 112.5 jit_solution(8649688726684760439)
XLA Ops:
  1.8 2.6 %collective-permute-start = (f32[72,512]{1,0:T(8,128)S(1)}, f32[72,512]{1,0:T(8,128)S(1)}, u32[]{:S(2)}, u32[]{:S(2)}) collective-permute-start(f32[72,512]{1,0:T(8,128)S(1)} %get-tuple-element.177), channel_id=1, source_target_pairs={{0,1},{1,2},{2,3},{3,4},{4,5},{5,6},{6,7},{7,8},{8,9},{9,10},{10,1... | collective-permute-start | bytes 442376 | tf_op jit(solution)/shard_map/ppermute | solution.py:445
  4.6 4.1 %late_gates.1 = (bf16[512,512]{1,0:T(8,128)(2,1)S(1)}, f8e5m2[512,512]{1,0:T(32,128)(4,1)S(1)}, f8e5m2[512,512]{1,0:T(32,128)(4,1)S(1)}, bf16[512,512]{1,0:T(8,1...) custom-call(f32[1024,512]{1,0:T(8,128)S(1)} %copy-done.13, ...), custom_call_target="tpu_custom_call" | custom-call | flops 11600000000 | bytes 1 | tf_op jit(solution)/shard_map/late_gates/pallas_call | solution.py:72
  8.7 4.3 %early_gates.1 = (bf16[512,512]{1,0:T(8,128)(2,1)S(1)}, f8e5m2[512,512]{1,0:T(32,128)(4,1)S(1)}, f8e5m2[512,512]{1,0:T(32,128)(4,1)S(1)}, bf16[512,128]{1,0:T(8,...) custom-call(f32[72,512]{1,0:T(8,128)S(1)} %collective-permute-done.r, ...), custom_call_target="tpu_custom_call" | custom-call | flops 12760000512 | bytes 1 | tf_op jit(solution)/shard_map/early_gates/pallas_call | solution.py:72
  14.4 2.7 %collective-permute-start.1 = (f32[256,8,128]{2,1,0:T(8,128)S(1)}, f32[256,8,128]{2,1,0:T(8,128)S(1)}, u32[]{:S(2)}, u32[]{:S(2)}) collective-permute-start(f32[256,8,128]{2,1,0:T(8,128)S(1)} %get-tuple-element.211), channel_id=1, source_target_pairs={{0,1},{1,0},{2,3},{3,2},{4,5},{5,4},{6,7},{7,6},{8,9},{9,8},{10,11... | collective-permute-start | bytes 3145736 | tf_op jit(solution)/shard_map/ppermute | solution.py:211
  17.1 3.3 %gate_grad.1 = (bf16[1024,1024]{1,0:T(8,128)(2,1)S(1)}, f8e5m2[1024,1024]{1,0:T(32,128)(4,1)S(1)}, f8e5m2[1024,1024]{1,0:T(32,128)(4,1)S(1)}, f32[8,128]{1,0:T(8,128)S(1)}) custom-call(bf16[1024,1024]{1,0:T(8,128)(2,1)S(1)} %get-tuple-element.197.refs_6_.refs_0_, f8e4m3fn[1024,1024]{1,0:T(32,128)(4,1)S(1)} %get-tuple-element.198.refs_7_.refs_1_, ...), custom_call_target="tpu_custom_call" | custom-call | flops 9859999744 | bytes 1 | tf_op jit(solution)/shard_map/gate_grad/pallas_call | solution.py:72
  34.6 3.4 %do_sg.2 = (f32[1024,512]{1,0:T(8,128)}, f32[8,128]{1,0:T(8,128)S(1)}) custom-call(bf16[1024,1024]{1,0:T(8,128)(2,1)S(1)} %get-tuple-element.206.refs_6_.refs_0_, f8e5m2[1024,1024]{1,0:T(32,128)(4,1)S(1)} %get-tuple-element.207.refs_7_.refs_1_, f8e5m2[1024,1024]{1,0:T(32,128)(4,1)S(1)} %get-tuple-element.208.refs_8_.refs_2_, ...), custom_call_target="tpu_custom_call" | custom-call | flops 10149999616 | bytes 1 | tf_op jit(solution)/shard_map/do_sg/pallas_call | solution.py:72
  38.0 2.6 %collective-permute-done.6.refs_1_ = f32[64,8,128]{2,1,0:T(8,128)S(1)} collective-permute-done((f32[64,8,128]{2,1,0:T(8,128)S(1)}, f32[64,8,128]{2,1,0:T(8,128)S(1)}, u32[]{:S(2)}, u32[]{:S(2)}) %collective-permute-start.6) | collective-permute-done | bytes 262176 | tf_op jit(solution)/shard_map/ppermute | solution.py:211
  45.5 2.2 %do_mix.2 = (f32[1024,512]{1,0:T(8,128)}, f32[1024,512]{1,0:T(8,128)}, f32[8,128]{1,0:T(8,128)S(1)}) custom-call(bf16[512,512]{1,0:T(8,128)(2,1)S(1)} %get-tuple-element.188.refs_0_, f8e4m3fn[512,512]{1,0:T(32,128)(4,1)S(1)} %get-tuple-element.189.refs_1_, f8e4m3fn[512,512]{1,0:T(32,128)(4,1)S(1)} %get-tuple-element.190.refs_2_, ...), custom_call_target="tpu_custom_call" | custom-call | flops 6380000256 | bytes 1 | tf_op jit(solution)/shard_map/do_mix/pallas_call | solution.py:72
  47.8 4.4 %collective-permute-done.8.refs_1_ = f32[64,8,128]{2,1,0:T(8,128)S(1)} collective-permute-done((f32[64,8,128]{2,1,0:T(8,128)S(1)}, f32[64,8,128]{2,1,0:T(8,128)S(1)}, u32[]{:S(2)}, u32[]{:S(2)}) %collective-permute-start.8) | collective-permute-done | bytes 262176 | tf_op jit(solution)/shard_map/ppermute | solution.py:211
  52.2 3.0 %collective-permute-start.12 = (f32[64,8,128]{2,1,0:T(8,128)S(1)}, f32[64,8,128]{2,1,0:T(8,128)S(1)}, u32[]{:S(2)}, u32[]{:S(2)}) collective-permute-start(f32[64,8,128]{2,1,0:T(8,128)S(1)} %get-tuple-element.261.refs_0_), channel_id=1, source_target_pairs={{0,16},{1,9},{2,18},{3,11},{4,20},{5,13},{6,22},{7,15},{8,24},{9,1... | collective-permute-start | bytes 786440 | tf_op jit(solution)/shard_map/ppermute | solution.py:211
  55.6 2.2 %do_mix.3 = (f32[1024,512]{1,0:T(8,128)}, f32[1024,512]{1,0:T(8,128)}, f32[8,128]{1,0:T(8,128)S(1)}) custom-call(bf16[512,512]{1,0:T(8,128)(2,1)S(1)} %get-tuple-element.174.refs_3_.refs_0_, f8e4m3fn[512,512]{1,0:T(32,128)(4,1)S(1)} %get-tuple-element.175.refs_4_.refs_1_, ...), custom_call_target="tpu_custom_call", output_to_operand_aliasing={{0}: (8, {}), {1}: (9, {})} | custom-call | flops 6380000256 | bytes 1 | tf_op jit(solution)/shard_map/do_mix/pallas_call | solution.py:72
  59.8 2.5 %collective-permute-done.13.refs_1_ = f32[76,8,128]{2,1,0:T(8,128)S(1)} collective-permute-done((f32[76,8,128]{2,1,0:T(8,128)S(1)}, f32[76,8,128]{2,1,0:T(8,128)S(1)}, u32[]{:S(2)}, u32[]{:S(2)}) %collective-permute-start.13) | collective-permute-done | bytes 311328 | tf_op jit(solution)/shard_map/ppermute | solution.py:211
  62.3 2.5 %collective-permute-start.15 = (f32[38,8,128]{2,1,0:T(8,128)S(1)}, f32[38,8,128]{2,1,0:T(8,128)S(1)}, u32[]{:S(2)}, u32[]{:S(2)}) collective-permute-start(f32[38,8,128]{2,1,0:T(8,128)S(1)} %get-tuple-element.269), channel_id=1, source_target_pairs={{0,8},{1,17},{2,10},{3,19},{4,12},{5,21},{6,14},{7,23},{8,0},{9,25... | collective-permute-start | bytes 466952 | tf_op jit(solution)/shard_map/ppermute | solution.py:211
  66.2 2.8 %collective-permute-done.15.refs_1_ = f32[38,8,128]{2,1,0:T(8,128)S(1)} collective-permute-done((f32[38,8,128]{2,1,0:T(8,128)S(1)}, f32[38,8,128]{2,1,0:T(8,128)S(1)}, u32[]{:S(2)}, u32[]{:S(2)}) %collective-permute-start.15) | collective-permute-done | bytes 155680 | tf_op jit(solution)/shard_map/ppermute | solution.py:211
  71.0 2.5 %collective-permute-done.14.refs_1_ = f32[32,8,128]{2,1,0:T(8,128)S(1)} collective-permute-done((f32[32,8,128]{2,1,0:T(8,128)S(1)}, f32[32,8,128]{2,1,0:T(8,128)S(1)}, u32[]{:S(2)}, u32[]{:S(2)}) %collective-permute-start.14) | collective-permute-done | bytes 131104 | tf_op jit(solution)/shard_map/ppermute | solution.py:211
  73.7 2.1 %collective-permute-start.29 = (f32[128,8,128]{2,1,0:T(8,128)S(1)}, f32[128,8,128]{2,1,0:T(8,128)S(1)}, u32[]{:S(2)}, u32[]{:S(2)}) collective-permute-start(f32[128,8,128]{2,1,0:T(8,128)S(1)} %get-tuple-element.287.refs_0_), channel_id=1, source_target_pairs={{0,4},{1,3},{2,6},{3,1},{4,0},{5,7},{6,2},{7,5},{8,12},{9,11},{10,... | collective-permute-start | bytes 1572872 | tf_op jit(solution)/shard_map/ppermute | solution.py:211
  79.7 2.2 %collective-permute-start.19 = (f32[64,8,128]{2,1,0:T(8,128)S(1)}, f32[64,8,128]{2,1,0:T(8,128)S(1)}, u32[]{:S(2)}, u32[]{:S(2)}) collective-permute-start(f32[64,8,128]{2,1,0:T(8,128)S(1)} %get-tuple-element.281.refs_0_), channel_id=1, source_target_pairs={{0,8},{1,17},{2,10},{3,19},{4,12},{5,21},{6,14},{7,23},{8,0},{9,25... | collective-permute-start | bytes 786440 | tf_op jit(solution)/shard_map/ppermute | solution.py:211
  81.9 3.5 %do_sg.3 = (f32[1024,512]{1,0:T(8,128)}, f32[7,80]{1,0:T(8,128)}, f32[8,128]{1,0:T(8,128)S(1)}) custom-call(bf16[1024,1024]{1,0:T(8,128)(2,1)S(1)} %get-tuple-element.206.refs_6_.refs_0_, f8e5m2[1024,1024]{1,0:T(32,128)(4,1)S(1)} %get-tuple-element.207.refs_7_.refs_1_, ...), custom_call_target="tpu_custom_call", output_to_operand_aliasing={{0}: (10, {})} | custom-call | flops 10149999616 | bytes 1 | tf_op jit(solution)/shard_map/do_sg/pallas_call | solution.py:72
  87.6 3.0 %collective-permute-start.26 = (f32[128,8,128]{2,1,0:T(8,128)S(1)}, f32[128,8,128]{2,1,0:T(8,128)S(1)}, u32[]{:S(2)}, u32[]{:S(2)}) collective-permute-start(f32[128,8,128]{2,1,0:T(8,128)S(1)} %get-tuple-element.285.refs_8_), channel_id=1, source_target_pairs={{0,4},{1,3},{2,6},{3,1},{4,0},{5,7},{6,2},{7,5},{8,12},{9,11},{10,... | collective-permute-start | bytes 1572872 | tf_op jit(solution)/shard_map/ppermute | solution.py:211
  93.8 4.0 %collective-permute-done.26.refs_0_ = f32[128,8,128]{2,1,0:T(8,128)S(1)} collective-permute-done((f32[128,8,128]{2,1,0:T(8,128)S(1)}, f32[128,8,128]{2,1,0:T(8,128)S(1)}, u32[]{:S(2)}, u32[]{:S(2)}) %collective-permute-start.26) | collective-permute-done | bytes 524320 | tf_op jit(solution)/shard_map/ppermute | solution.py:211
  98.1 2.2 %do_u1_u1.1 = (f32[512,1024]{1,0:T(8,128)}, f32[512,1024]{1,0:T(8,128)}, f32[512,1024]{1,0:T(8,128)}, bf16[512,1024]{1,0:T(8,128)(2,1)}, f32[2,512,1024]{2,1,0:T...) custom-call(f32[128,8,128]{2,1,0:T(8,128)S(1)} %collective-permute-d, ...), custom_call_target="tpu_custom_call", output_to_operand_aliasing={{0}: (4, {}), {1}: (5, {}), {2}: (6, {}), {3}: (7, {})} | custom-call | flops 6089999872 | bytes 1 | tf_op jit(solution)/shard_map/do_u1_u1/pallas_call | solution.py:72
  100.3 4.1 %collective-permute-done.24.refs_3_.refs_20_ = f32[152,8,128]{2,1,0:T(8,128)S(1)} collective-permute-done((f32[152,8,128]{2,1,0:T(8,128)S(1)}, f32[152,8,128]{2,1,0:T(8,128)S(1)}, u32[]{:S(2)}, u32[]{:S(2)}) %collective-permute-start.24) | collective-permute-done | bytes 622624 | tf_op jit(solution)/shard_map/ppermute | solution.py:211
  104.6 3.2 %do_u4.1 = (f32[2,512,1024]{2,1,0:T(8,128)}, f32[2,512,1024]{2,1,0:T(8,128)}, f32[2,512,1024]{2,1,0:T(8,128)}, bf16[2,512,1024]{2,1,0:T(8,128)(2,1)}, f32[8,128]{1,0:T(8,128)S(1)}) custom-call(f32[128,8,128]{2,1,0:T(8,128)S(1)} %collective-permute-done.26.refs_0_, ...), custom_call_target="tpu_custom_call", output_to_operand_aliasing={{0}: (7, {}), {1}: (8, {}), {2}: (9, {}), {3}: (10, {})} | custom-call | flops 9280000000 | bytes 1 | tf_op jit(solution)/shard_map/do_u4/pallas_call | solution.py:72
  107.9 4.4 %do_u3_u1_few.1 = (f32[2,512,1024]{2,1,0:T(8,128)}, f32[2,512,1024]{2,1,0:T(8,128)}, f32[2,512,1024]{2,1,0:T(8,128)}, bf16[2,512,1024]{2,1,0:T(8,128)(2,1)}, f32...) custom-call(f32[128,8,128]{2,1,0:T(8,128)S(1)} %collective-permute-d, ...), custom_call_target="tpu_custom_call", output_to_operand_aliasing={{0}: (6, {}), {1}: (7, {}), {2}: (8, {}), {3}: (9, {}), {4}... | custom-call | flops 11889999872 | bytes 1 | tf_op jit(solution)/shard_map/do_u3_u1_few/pallas_call | solution.py:72
  (113 shorter events, 37.1 us)
Async XLA Ops:
  14.4 7.5 %collective-permute-start.1 = (f32[256,8,128]{2,1,0:T(8,128)S(1)}, f32[256,8,128]{2,1,0:T(8,128)S(1)}, u32[]{:S(2)}, u32[]{:S(2)}) collective-permute-start(f32[256,8,128]{2,1,0:T(8,128)S(1)} %get-tuple-element.211), channel_id=1, source_target_pairs={{0,1},{1,0},{2,3},{3,2},{4,5},{5,4},{6,7},{7,6},{8,9},{9,8},{10,11... | collective-permute-start | bytes 3145736 | tf_op jit(solution)/shard_map/ppermute | solution.py:211
  22.0 9.2 %collective-permute-start.3 = (f32[128,8,128]{2,1,0:T(8,128)S(1)}, f32[128,8,128]{2,1,0:T(8,128)S(1)}, u32[]{:S(2)}, u32[]{:S(2)}) collective-permute-start(f32[128,8,128]{2,1,0:T(8,128)S(1)} %get-tuple-element.218), channel_id=1, source_target_pairs={{0,4},{1,3},{2,6},{3,1},{4,0},{5,7},{6,2},{7,5},{8,12},{9,11},{10,... | collective-permute-start | bytes 1572872 | tf_op jit(solution)/shard_map/ppermute | solution.py:211
  24.9 7.9 %collective-permute-start.2 = (f32[256,8,128]{2,1,0:T(8,128)S(1)}, f32[256,8,128]{2,1,0:T(8,128)S(1)}, u32[]{:S(2)}, u32[]{:S(2)}) collective-permute-start(f32[256,8,128]{2,1,0:T(8,128)S(1)} %get-tuple-element.216), channel_id=1, source_target_pairs={{0,1},{1,0},{2,3},{3,2},{4,5},{5,4},{6,7},{7,6},{8,9},{9,8},{10,11... | collective-permute-start | bytes 3145736 | tf_op jit(solution)/shard_map/ppermute | solution.py:211
  28.4 14.3 %collective-permute-start.5 = (f32[304,8,128]{2,1,0:T(8,128)S(1)}, f32[304,8,128]{2,1,0:T(8,128)S(1)}, u32[]{:S(2)}, u32[]{:S(2)}) collective-permute-start(f32[304,8,128]{2,1,0:T(8,128)S(1)} %get-tuple-element.234), channel_id=1, source_target_pairs={{0,1},{1,0},{2,3},{3,2},{4,5},{5,4},{6,7},{7,6},{8,9},{9,8},{10,11... | collective-permute-start | bytes 3735560 | tf_op jit(solution)/shard_map/ppermute | solution.py:211
  31.3 9.2 %collective-permute-start.6 = (f32[64,8,128]{2,1,0:T(8,128)S(1)}, f32[64,8,128]{2,1,0:T(8,128)S(1)}, u32[]{:S(2)}, u32[]{:S(2)}) collective-permute-start(f32[64,8,128]{2,1,0:T(8,128)S(1)} %get-tuple-element.236), channel_id=1, source_target_pairs={{0,2},{1,5},{2,0},{3,7},{4,6},{5,1},{6,4},{7,3},{8,10},{9,13},{10,... | collective-permute-start | bytes 786440 | tf_op jit(solution)/shard_map/ppermute | solution.py:211
  33.0 11.8 %collective-permute-start.4 = (f32[128,8,128]{2,1,0:T(8,128)S(1)}, f32[128,8,128]{2,1,0:T(8,128)S(1)}, u32[]{:S(2)}, u32[]{:S(2)}) collective-permute-start(f32[128,8,128]{2,1,0:T(8,128)S(1)} %get-tuple-element.231), channel_id=1, source_target_pairs={{0,4},{1,3},{2,6},{3,1},{4,0},{5,7},{6,2},{7,5},{8,12},{9,11},{10,... | collective-permute-start | bytes 1572872 | tf_op jit(solution)/shard_map/ppermute | solution.py:211
  40.6 11.6 %collective-permute-start.8 = (f32[64,8,128]{2,1,0:T(8,128)S(1)}, f32[64,8,128]{2,1,0:T(8,128)S(1)}, u32[]{:S(2)}, u32[]{:S(2)}) collective-permute-start(f32[64,8,128]{2,1,0:T(8,128)S(1)} %get-tuple-element.247.refs_0_), channel_id=1, source_target_pairs={{0,8},{1,17},{2,10},{3,19},{4,12},{5,21},{6,14},{7,23},{8,0},{9,25... | collective-permute-start | bytes 786440 | tf_op jit(solution)/shard_map/ppermute | solution.py:211
  42.9 12.4 %collective-permute-start.7 = (f32[152,8,128]{2,1,0:T(8,128)S(1)}, f32[152,8,128]{2,1,0:T(8,128)S(1)}, u32[]{:S(2)}, u32[]{:S(2)}) collective-permute-start(f32[152,8,128]{2,1,0:T(8,128)S(1)} %get-tuple-element.246), channel_id=1, source_target_pairs={{0,4},{1,3},{2,6},{3,1},{4,0},{5,7},{6,2},{7,5},{8,12},{9,11},{10,... | collective-permute-start | bytes 1867784 | tf_op jit(solution)/shard_map/ppermute | solution.py:211
  44.9 14.2 %collective-permute-start.10 = (f32[64,8,128]{2,1,0:T(8,128)S(1)}, f32[64,8,128]{2,1,0:T(8,128)S(1)}, u32[]{:S(2)}, u32[]{:S(2)}) collective-permute-start(f32[64,8,128]{2,1,0:T(8,128)S(1)} %get-tuple-element.257), channel_id=1, source_target_pairs={{0,8},{1,17},{2,10},{3,19},{4,12},{5,21},{6,14},{7,23},{8,0},{9,25... | collective-permute-start | bytes 786440 | tf_op jit(solution)/shard_map/ppermute | solution.py:211
  52.2 12.8 %collective-permute-start.12 = (f32[64,8,128]{2,1,0:T(8,128)S(1)}, f32[64,8,128]{2,1,0:T(8,128)S(1)}, u32[]{:S(2)}, u32[]{:S(2)}) collective-permute-start(f32[64,8,128]{2,1,0:T(8,128)S(1)} %get-tuple-element.261.refs_0_), channel_id=1, source_target_pairs={{0,16},{1,9},{2,18},{3,11},{4,20},{5,13},{6,22},{7,15},{8,24},{9,1... | collective-permute-start | bytes 786440 | tf_op jit(solution)/shard_map/ppermute | solution.py:211
  59.1 7.0 %collective-permute-start.11 = (f32[32,8,128]{2,1,0:T(8,128)S(1)}, f32[32,8,128]{2,1,0:T(8,128)S(1)}, u32[]{:S(2)}, u32[]{:S(2)}) collective-permute-start(f32[32,8,128]{2,1,0:T(8,128)S(1)} %get-tuple-element.260), channel_id=1, source_target_pairs={{0,2},{1,5},{2,0},{3,7},{4,6},{5,1},{6,4},{7,3},{8,10},{9,13},{10,... | collective-permute-start | bytes 393224 | tf_op jit(solution)/shard_map/ppermute | solution.py:211
  65.0 8.5 %collective-permute-start.18 = (f32[64,8,128]{2,1,0:T(8,128)S(1)}, f32[64,8,128]{2,1,0:T(8,128)S(1)}, u32[]{:S(2)}, u32[]{:S(2)}) collective-permute-start(f32[64,8,128]{2,1,0:T(8,128)S(1)} %get-tuple-element.274.refs_0_), channel_id=1, source_target_pairs={{0,2},{1,5},{2,0},{3,7},{4,6},{5,1},{6,4},{7,3},{8,10},{9,13},{10,... | collective-permute-start | bytes 786440 | tf_op jit(solution)/shard_map/ppermute | solution.py:211
  66.2 7.3 %collective-permute-start.14 = (f32[32,8,128]{2,1,0:T(8,128)S(1)}, f32[32,8,128]{2,1,0:T(8,128)S(1)}, u32[]{:S(2)}, u32[]{:S(2)}) collective-permute-start(f32[32,8,128]{2,1,0:T(8,128)S(1)} %get-tuple-element.267.refs_0_), channel_id=1, source_target_pairs={{0,16},{1,9},{2,18},{3,11},{4,20},{5,13},{6,22},{7,15},{8,24},{9,1... | collective-permute-start | bytes 393224 | tf_op jit(solution)/shard_map/ppermute | solution.py:211
  69.5 12.3 %collective-permute-start.9 = (f32[72,512]{1,0:T(8,128)S(1)}, f32[72,512]{1,0:T(8,128)S(1)}, u32[]{:S(2)}, u32[]{:S(2)}) collective-permute-start(f32[72,512]{1,0:T(8,128)S(1)} %get-tuple-element.253), channel_id=1, source_target_pairs={{1,0},{2,1},{3,2},{4,3},{5,4},{6,5},{7,6},{8,7},{9,8},{10,9},{11,1... | collective-permute-start | bytes 442376 | tf_op jit(solution)/shard_map/ppermute | solution.py:582
  73.7 16.9 %collective-permute-start.29 = (f32[128,8,128]{2,1,0:T(8,128)S(1)}, f32[128,8,128]{2,1,0:T(8,128)S(1)}, u32[]{:S(2)}, u32[]{:S(2)}) collective-permute-start(f32[128,8,128]{2,1,0:T(8,128)S(1)} %get-tuple-element.287.refs_0_), channel_id=1, source_target_pairs={{0,4},{1,3},{2,6},{3,1},{4,0},{5,7},{6,2},{7,5},{8,12},{9,11},{10,... | collective-permute-start | bytes 1572872 | tf_op jit(solution)/shard_map/ppermute | solution.py:211
  75.8 14.8 %collective-permute-start.23 = (f32[128,8,128]{2,1,0:T(8,128)S(1)}, f32[128,8,128]{2,1,0:T(8,128)S(1)}, u32[]{:S(2)}, u32[]{:S(2)}) collective-permute-start(f32[128,8,128]{2,1,0:T(8,128)S(1)} %get-tuple-element.287.refs_0_), channel_id=1, source_target_pairs={{0,1},{1,0},{2,3},{3,2},{4,5},{5,4},{6,7},{7,6},{8,9},{9,8},{10,11... | collective-permute-start | bytes 1572872 | tf_op jit(solution)/shard_map/ppermute | solution.py:211
  75.8 9.5 %collective-permute-start.20 = (f32[38,8,128]{2,1,0:T(8,128)S(1)}, f32[38,8,128]{2,1,0:T(8,128)S(1)}, u32[]{:S(2)}, u32[]{:S(2)}) collective-permute-start(f32[38,8,128]{2,1,0:T(8,128)S(1)} %get-tuple-element.282.refs_0_), channel_id=1, source_target_pairs={{0,8},{1,17},{2,10},{3,19},{4,12},{5,21},{6,14},{7,23},{8,0},{9,25... | collective-permute-start | bytes 466952 | tf_op jit(solution)/shard_map/ppermute | solution.py:211
  79.7 7.8 %collective-permute-start.19 = (f32[64,8,128]{2,1,0:T(8,128)S(1)}, f32[64,8,128]{2,1,0:T(8,128)S(1)}, u32[]{:S(2)}, u32[]{:S(2)}) collective-permute-start(f32[64,8,128]{2,1,0:T(8,128)S(1)} %get-tuple-element.281.refs_0_), channel_id=1, source_target_pairs={{0,8},{1,17},{2,10},{3,19},{4,12},{5,21},{6,14},{7,23},{8,0},{9,25... | collective-permute-start | bytes 786440 | tf_op jit(solution)/shard_map/ppermute | solution.py:211
  85.4 7.7 %collective-permute-start.22 = (f32[76,8,128]{2,1,0:T(8,128)S(1)}, f32[76,8,128]{2,1,0:T(8,128)S(1)}, u32[]{:S(2)}, u32[]{:S(2)}) collective-permute-start(f32[76,8,128]{2,1,0:T(8,128)S(1)} %get-tuple-element.286.refs_0_), channel_id=1, source_target_pairs={{0,2},{1,5},{2,0},{3,7},{4,6},{5,1},{6,4},{7,3},{8,10},{9,13},{10,... | collective-permute-start | bytes 933896 | tf_op jit(solution)/shard_map/ppermute | solution.py:211
  87.6 10.2 %collective-permute-start.26 = (f32[128,8,128]{2,1,0:T(8,128)S(1)}, f32[128,8,128]{2,1,0:T(8,128)S(1)}, u32[]{:S(2)}, u32[]{:S(2)}) collective-permute-start(f32[128,8,128]{2,1,0:T(8,128)S(1)} %get-tuple-element.285.refs_8_), channel_id=1, source_target_pairs={{0,4},{1,3},{2,6},{3,1},{4,0},{5,7},{6,2},{7,5},{8,12},{9,11},{10,... | collective-permute-start | bytes 1572872 | tf_op jit(solution)/shard_map/ppermute | solution.py:211
  90.6 7.5 %collective-permute-start.30 = (f32[128,8,128]{2,1,0:T(8,128)S(1)}, f32[128,8,128]{2,1,0:T(8,128)S(1)}, u32[]{:S(2)}, u32[]{:S(2)}) collective-permute-start(f32[128,8,128]{2,1,0:T(8,128)S(1)} %collective-permute-done.29.refs_10_), channel_id=1, source_target_pairs={{0,1},{1,0},{2,3},{3,2},{4,5},{5,4},{6,7},{7,6},{8,9},{9,8},{10,11... | collective-permute-start | bytes 1572872 | tf_op jit(solution)/shard_map/ppermute | solution.py:211
  93.1 11.3 %collective-permute-start.24 = (f32[152,8,128]{2,1,0:T(8,128)S(1)}, f32[152,8,128]{2,1,0:T(8,128)S(1)}, u32[]{:S(2)}, u32[]{:S(2)}) collective-permute-start(f32[152,8,128]{2,1,0:T(8,128)S(1)} %get-tuple-element.290.refs_1_.refs_18_), channel_id=1, source_target_pairs={{0,4},{1,3},{2,6},{3,1},{4,0},{5,7},{6,2},{7,5},{8,12},{9,11},{10,... | collective-permute-start | bytes 1867784 | tf_op jit(solution)/shard_map/ppermute | solution.py:211
  93.2 11.3 %collective-permute-start.28 = (f32[152,8,128]{2,1,0:T(8,128)S(1)}, f32[152,8,128]{2,1,0:T(8,128)S(1)}, u32[]{:S(2)}, u32[]{:S(2)}) collective-permute-start(f32[152,8,128]{2,1,0:T(8,128)S(1)} %get-tuple-element.290.refs_1_.refs_18_), channel_id=1, source_target_pairs={{0,1},{1,0},{2,3},{3,2},{4,5},{5,4},{6,7},{7,6},{8,9},{9,8},{10,11... | collective-permute-start | bytes 1867784 | tf_op jit(solution)/shard_map/ppermute | solution.py:211
  93.5 14.3 %collective-permute-start.21 = (f32[128,8,128]{2,1,0:T(8,128)S(1)}, f32[128,8,128]{2,1,0:T(8,128)S(1)}, u32[]{:S(2)}, u32[]{:S(2)}) collective-permute-start(f32[128,8,128]{2,1,0:T(8,128)S(1)} %get-tuple-element.285.refs_8_), channel_id=1, source_target_pairs={{0,1},{1,0},{2,3},{3,2},{4,5},{5,4},{6,7},{7,6},{8,9},{9,8},{10,11... | collective-permute-start | bytes 1572872 | tf_op jit(solution)/shard_map/ppermute | solution.py:211
  (25 other events, 128.3 us)

commit v2 on v1

--- a/solution.py
+++ b/solution.py
@@ -810,8 +810,8 @@
 
 WHOLE = (2, 1, 1)
 SCRIPT = """
-jP gg kP P j0 k0 j1 k1 P 0 sg0 P 1 back 0 mix0 P 1 mix1 0 1 P 0 1 0 P 1 0 sP rP sg1 1 0 s0 =Pab 1 s1 r0 =Pd0a
-r1 =0cd1bc =0b1adPcf
+jP gg kP P j0 k0 j1 k1 P 0 sg0 P 1 back 0 mix0 P 1 mix1 0 1 P 0 1 0 P 1 0 sP rP sg1 1 0 s0 1 s1 =Pb r0 =0abPacd
+r1 =1a =0cd1bc =1df
 """
 
 

time: 114 us -> 112 us (0.982); the launches traced: 112 us -> 112 us
    pallas_call x39 -> x40, Pallas kernels: 47 us -> 47.9 us  [call(): pl.pallas_call(run, out_shape=[kinds[id(s)](*o) for o, s in zip(outs, out...]
  transfers between devices with their start and end apart: 31 -> 31, of which waited for: 13 -> 13; matrix products, arithmetic and copies ran while one was open for 0% -> 0% of each run, Pallas kernels for 32% -> 34%
where the time goes in v2:
time: 112 us
  Pallas kernels  47.9 us (43%)
  starting transfers between devices  34.3 us (31%)
  waiting for transfers between devices  28 us (25%)
  between operations  1.42 us (1%)
    pallas_call x40, Pallas kernels, call(): pl.pallas_call(run, out_shape=[kinds[id(s)](*o) for o, s in zip(outs, out...  47.9 us
    ppermute x29, starting transfers between devices, swap(): return lax.ppermute(x, axes, self.pairs[step])  30.2 us
    ppermute x29, waiting for transfers between devices, swap(): return lax.ppermute(x, axes, self.pairs[step])  28 us
    ppermute x1, starting transfers between devices, solve(): halo = lax.ppermute(packed, axes, [(i, i + 1) for i in range(count - 1)])  2.63 us
  transfers between devices with their start and end apart: 31, of which 13 were waited for; matrix products, arithmetic and copies ran while one was open for 0% of the time, Pallas kernels for 34%

profile of v2, /device:TPU:0, one launch (start us, length us, event | category | flops | bytes accessed | tf_op | source)
XLA Modules:
  0.0 111.7 jit_solution(944382072210068072)
XLA Ops:
  1.8 2.6 %collective-permute-start = (f32[72,512]{1,0:T(8,128)S(1)}, f32[72,512]{1,0:T(8,128)S(1)}, u32[]{:S(2)}, u32[]{:S(2)}) collective-permute-start(f32[72,512]{1,0:T(8,128)S(1)} %get-tuple-element.178), channel_id=1, source_target_pairs={{0,1},{1,2},{2,3},{3,4},{4,5},{5,6},{6,7},{7,8},{8,9},{9,10},{10,1... | collective-permute-start | bytes 442376 | tf_op jit(solution)/shard_map/ppermute | solution.py:445
  4.6 4.3 %late_gates.1 = (bf16[512,512]{1,0:T(8,128)(2,1)S(1)}, f8e5m2[512,512]{1,0:T(32,128)(4,1)S(1)}, f8e5m2[512,512]{1,0:T(32,128)(4,1)S(1)}, bf16[512,512]{1,0:T(8,1...) custom-call(f32[1024,512]{1,0:T(8,128)S(1)} %copy-done.10, ...), custom_call_target="tpu_custom_call" | custom-call | flops 11600000000 | bytes 1 | tf_op jit(solution)/shard_map/late_gates/pallas_call | solution.py:72
  8.9 4.4 %early_gates.1 = (bf16[512,512]{1,0:T(8,128)(2,1)S(1)}, f8e5m2[512,512]{1,0:T(32,128)(4,1)S(1)}, f8e5m2[512,512]{1,0:T(32,128)(4,1)S(1)}, bf16[512,128]{1,0:T(8,...) custom-call(f32[72,512]{1,0:T(8,128)S(1)} %collective-permute-done.r, ...), custom_call_target="tpu_custom_call" | custom-call | flops 12760000512 | bytes 1 | tf_op jit(solution)/shard_map/early_gates/pallas_call | solution.py:72
  14.6 2.7 %collective-permute-start.1 = (f32[256,8,128]{2,1,0:T(8,128)S(1)}, f32[256,8,128]{2,1,0:T(8,128)S(1)}, u32[]{:S(2)}, u32[]{:S(2)}) collective-permute-start(f32[256,8,128]{2,1,0:T(8,128)S(1)} %get-tuple-element.212), channel_id=1, source_target_pairs={{0,1},{1,0},{2,3},{3,2},{4,5},{5,4},{6,7},{7,6},{8,9},{9,8},{10,11... | collective-permute-start | bytes 3145736 | tf_op jit(solution)/shard_map/ppermute | solution.py:211
  17.3 3.3 %gate_grad.1 = (bf16[1024,1024]{1,0:T(8,128)(2,1)S(1)}, f8e5m2[1024,1024]{1,0:T(32,128)(4,1)S(1)}, f8e5m2[1024,1024]{1,0:T(32,128)(4,1)S(1)}, f32[8,128]{1,0:T(8,128)S(1)}) custom-call(bf16[1024,1024]{1,0:T(8,128)(2,1)S(1)} %get-tuple-element.198.refs_6_.refs_0_, f8e4m3fn[1024,1024]{1,0:T(32,128)(4,1)S(1)} %get-tuple-element.199.refs_7_.refs_1_, ...), custom_call_target="tpu_custom_call" | custom-call | flops 9859999744 | bytes 1 | tf_op jit(solution)/shard_map/gate_grad/pallas_call | solution.py:72
  26.6 2.0 %tap1_grad0.1 = (f32[304,8,128]{2,1,0:T(8,128)S(1)}, f32[4,24,8,128]{3,2,1,0:T(8,128)S(1)}, f32[16,1024]{1,0:T(8,128)S(1)}, f32[8,128]{1,0:T(8,128)S(1)}) custom-call(bf16[512,512]{1,0:T(8,128)(2,1)S(1)} %get-tuple-element.179.refs_2_.refs_0_, f8e5m2[512,512]{1,0:T(32,128)(4,1)S(1)} %get-tuple-element.180.refs_3_.refs_1_, ...), custom_call_target="tpu_custom_call" | custom-call | flops 5800000000 | bytes 1 | tf_op jit(solution)/shard_map/tap1_grad0/pallas_call | solution.py:72
  34.8 3.5 %do_sg.2 = (f32[1024,512]{1,0:T(8,128)}, f32[8,128]{1,0:T(8,128)S(1)}) custom-call(bf16[1024,1024]{1,0:T(8,128)(2,1)S(1)} %get-tuple-element.207.refs_6_.refs_0_, f8e5m2[1024,1024]{1,0:T(32,128)(4,1)S(1)} %get-tuple-element.208.refs_7_.refs_1_, f8e5m2[1024,1024]{1,0:T(32,128)(4,1)S(1)} %get-tuple-element.209.refs_8_.refs_2_, ...), custom_call_target="tpu_custom_call" | custom-call | flops 10149999616 | bytes 1 | tf_op jit(solution)/shard_map/do_sg/pallas_call | solution.py:72
  38.3 2.4 %collective-permute-done.6.refs_1_ = f32[64,8,128]{2,1,0:T(8,128)S(1)} collective-permute-done((f32[64,8,128]{2,1,0:T(8,128)S(1)}, f32[64,8,128]{2,1,0:T(8,128)S(1)}, u32[]{:S(2)}, u32[]{:S(2)}) %collective-permute-start.6) | collective-permute-done | bytes 262176 | tf_op jit(solution)/shard_map/ppermute | solution.py:211
  45.8 2.2 %do_mix.2 = (f32[1024,512]{1,0:T(8,128)}, f32[1024,512]{1,0:T(8,128)}, f32[8,128]{1,0:T(8,128)S(1)}) custom-call(bf16[512,512]{1,0:T(8,128)(2,1)S(1)} %get-tuple-element.189.refs_0_, f8e4m3fn[512,512]{1,0:T(32,128)(4,1)S(1)} %get-tuple-element.190.refs_1_, f8e4m3fn[512,512]{1,0:T(32,128)(4,1)S(1)} %get-tuple-element.191.refs_2_, ...), custom_call_target="tpu_custom_call" | custom-call | flops 6380000256 | bytes 1 | tf_op jit(solution)/shard_map/do_mix/pallas_call | solution.py:72
  48.0 4.4 %collective-permute-done.8.refs_1_ = f32[64,8,128]{2,1,0:T(8,128)S(1)} collective-permute-done((f32[64,8,128]{2,1,0:T(8,128)S(1)}, f32[64,8,128]{2,1,0:T(8,128)S(1)}, u32[]{:S(2)}, u32[]{:S(2)}) %collective-permute-start.8) | collective-permute-done | bytes 262176 | tf_op jit(solution)/shard_map/ppermute | solution.py:211
  52.5 2.5 %collective-permute-start.12 = (f32[64,8,128]{2,1,0:T(8,128)S(1)}, f32[64,8,128]{2,1,0:T(8,128)S(1)}, u32[]{:S(2)}, u32[]{:S(2)}) collective-permute-start(f32[64,8,128]{2,1,0:T(8,128)S(1)} %get-tuple-element.262.refs_0_), channel_id=1, source_target_pairs={{0,16},{1,9},{2,18},{3,11},{4,20},{5,13},{6,22},{7,15},{8,24},{9,1... | collective-permute-start | bytes 786440 | tf_op jit(solution)/shard_map/ppermute | solution.py:211
  55.9 2.2 %do_mix.3 = (f32[1024,512]{1,0:T(8,128)}, f32[1024,512]{1,0:T(8,128)}, f32[8,128]{1,0:T(8,128)S(1)}) custom-call(bf16[512,512]{1,0:T(8,128)(2,1)S(1)} %get-tuple-element.175.refs_3_.refs_0_, f8e4m3fn[512,512]{1,0:T(32,128)(4,1)S(1)} %get-tuple-element.176.refs_4_.refs_1_, ...), custom_call_target="tpu_custom_call", output_to_operand_aliasing={{0}: (8, {}), {1}: (9, {})} | custom-call | flops 6380000256 | bytes 1 | tf_op jit(solution)/shard_map/do_mix/pallas_call | solution.py:72
  62.0 2.5 %collective-permute-start.15 = (f32[38,8,128]{2,1,0:T(8,128)S(1)}, f32[38,8,128]{2,1,0:T(8,128)S(1)}, u32[]{:S(2)}, u32[]{:S(2)}) collective-permute-start(f32[38,8,128]{2,1,0:T(8,128)S(1)} %get-tuple-element.270), channel_id=1, source_target_pairs={{0,8},{1,17},{2,10},{3,19},{4,12},{5,21},{6,14},{7,23},{8,0},{9,25... | collective-permute-start | bytes 466952 | tf_op jit(solution)/shard_map/ppermute | solution.py:211
  66.3 2.6 %collective-permute-done.15.refs_1_ = f32[38,8,128]{2,1,0:T(8,128)S(1)} collective-permute-done((f32[38,8,128]{2,1,0:T(8,128)S(1)}, f32[38,8,128]{2,1,0:T(8,128)S(1)}, u32[]{:S(2)}, u32[]{:S(2)}) %collective-permute-start.15) | collective-permute-done | bytes 155680 | tf_op jit(solution)/shard_map/ppermute | solution.py:211
  70.9 2.7 %collective-permute-done.14.refs_1_ = f32[32,8,128]{2,1,0:T(8,128)S(1)} collective-permute-done((f32[32,8,128]{2,1,0:T(8,128)S(1)}, f32[32,8,128]{2,1,0:T(8,128)S(1)}, u32[]{:S(2)}, u32[]{:S(2)}) %collective-permute-start.14) | collective-permute-done | bytes 131104 | tf_op jit(solution)/shard_map/ppermute | solution.py:211
  77.3 2.6 %collective-permute-done.16.refs_1_ = f32[32,8,128]{2,1,0:T(8,128)S(1)} collective-permute-done((f32[32,8,128]{2,1,0:T(8,128)S(1)}, f32[32,8,128]{2,1,0:T(8,128)S(1)}, u32[]{:S(2)}, u32[]{:S(2)}) %collective-permute-start.16) | collective-permute-done | bytes 131104 | tf_op jit(solution)/shard_map/ppermute | solution.py:211
  80.5 3.5 %do_sg.3 = (f32[1024,512]{1,0:T(8,128)}, f32[7,80]{1,0:T(8,128)}, f32[8,128]{1,0:T(8,128)S(1)}) custom-call(bf16[1024,1024]{1,0:T(8,128)(2,1)S(1)} %get-tuple-element.207.refs_6_.refs_0_, f8e5m2[1024,1024]{1,0:T(32,128)(4,1)S(1)} %get-tuple-element.208.refs_7_.refs_1_, ...), custom_call_target="tpu_custom_call", output_to_operand_aliasing={{0}: (10, {})} | custom-call | flops 10149999616 | bytes 1 | tf_op jit(solution)/shard_map/do_sg/pallas_call | solution.py:72
  84.1 2.2 %collective-permute-start.20 = (f32[76,8,128]{2,1,0:T(8,128)S(1)}, f32[76,8,128]{2,1,0:T(8,128)S(1)}, u32[]{:S(2)}, u32[]{:S(2)}) collective-permute-start(f32[76,8,128]{2,1,0:T(8,128)S(1)} %get-tuple-element.284.refs_0_), channel_id=1, source_target_pairs={{0,2},{1,5},{2,0},{3,7},{4,6},{5,1},{6,4},{7,3},{8,10},{9,13},{10,... | collective-permute-start | bytes 933896 | tf_op jit(solution)/shard_map/ppermute | solution.py:211
  86.2 2.4 %collective-permute-done.21.refs_1_ = f32[64,8,128]{2,1,0:T(8,128)S(1)} collective-permute-done((f32[64,8,128]{2,1,0:T(8,128)S(1)}, f32[64,8,128]{2,1,0:T(8,128)S(1)}, u32[]{:S(2)}, u32[]{:S(2)}) %collective-permute-start.21) | collective-permute-done | bytes 262176 | tf_op jit(solution)/shard_map/ppermute | solution.py:211
  88.7 3.0 %collective-permute-start.24 = (f32[128,8,128]{2,1,0:T(8,128)S(1)}, f32[128,8,128]{2,1,0:T(8,128)S(1)}, u32[]{:S(2)}, u32[]{:S(2)}) collective-permute-start(f32[128,8,128]{2,1,0:T(8,128)S(1)} %get-tuple-element.289.refs_0_), channel_id=1, source_target_pairs={{0,4},{1,3},{2,6},{3,1},{4,0},{5,7},{6,2},{7,5},{8,12},{9,11},{10,... | collective-permute-start | bytes 1572872 | tf_op jit(solution)/shard_map/ppermute | solution.py:211
  95.0 3.9 %collective-permute-done.24.refs_0_ = f32[128,8,128]{2,1,0:T(8,128)S(1)} collective-permute-done((f32[128,8,128]{2,1,0:T(8,128)S(1)}, f32[128,8,128]{2,1,0:T(8,128)S(1)}, u32[]{:S(2)}, u32[]{:S(2)}) %collective-permute-start.24) | collective-permute-done | bytes 524320 | tf_op jit(solution)/shard_map/ppermute | solution.py:211
  98.9 3.9 %do_u2_u3.1 = (f32[2,512,1024]{2,1,0:T(8,128)}, f32[2,512,1024]{2,1,0:T(8,128)}, f32[2,512,1024]{2,1,0:T(8,128)}, bf16[2,512,1024]{2,1,0:T(8,128)(2,1)}, f32[512...) custom-call(f32[128,8,128]{2,1,0:T(8,128)S(1)} %get-tuple-element.28, ...), custom_call_target="tpu_custom_call", output_to_operand_aliasing={{4}: (11, {}), {5}: (12, {}), {6}: (13, {}), {7}: (14, {})} | custom-call | flops 11310000128 | bytes 1 | tf_op jit(solution)/shard_map/do_u2_u3/pallas_call | solution.py:72
  105.6 3.3 %do_u4.1 = (f32[2,512,1024]{2,1,0:T(8,128)}, f32[2,512,1024]{2,1,0:T(8,128)}, f32[2,512,1024]{2,1,0:T(8,128)}, bf16[2,512,1024]{2,1,0:T(8,128)(2,1)}, f32[8,128]{1,0:T(8,128)S(1)}) custom-call(f32[128,8,128]{2,1,0:T(8,128)S(1)} %collective-permute-done.24.refs_0_, ...), custom_call_target="tpu_custom_call", output_to_operand_aliasing={{0}: (7, {}), {1}: (8, {}), {2}: (9, {}), {3}: (10, {})} | custom-call | flops 9280000000 | bytes 1 | tf_op jit(solution)/shard_map/do_u4/pallas_call | solution.py:72
  108.9 2.6 %do_u1_few.1 = (f32[2,512,1024]{2,1,0:T(8,128)}, f32[2,512,1024]{2,1,0:T(8,128)}, f32[2,512,1024]{2,1,0:T(8,128)}, bf16[2,512,1024]{2,1,0:T(8,128)(2,1)}, f32[80...) custom-call(f32[152,8,128]{2,1,0:T(8,128)S(1)} %collective-permute-d, ...), custom_call_target="tpu_custom_call", output_to_operand_aliasing={{0}: (4, {}), {1}: (5, {}), {2}: (6, {}), {3}: (7, {})} | custom-call | flops 6380000256 | bytes 1 | tf_op jit(solution)/shard_map/do_u1_few/pallas_call | solution.py:72
  (114 shorter events, 38.5 us)
Async XLA Ops:
  14.6 7.5 %collective-permute-start.1 = (f32[256,8,128]{2,1,0:T(8,128)S(1)}, f32[256,8,128]{2,1,0:T(8,128)S(1)}, u32[]{:S(2)}, u32[]{:S(2)}) collective-permute-start(f32[256,8,128]{2,1,0:T(8,128)S(1)} %get-tuple-element.212), channel_id=1, source_target_pairs={{0,1},{1,0},{2,3},{3,2},{4,5},{5,4},{6,7},{7,6},{8,9},{9,8},{10,11... | collective-permute-start | bytes 3145736 | tf_op jit(solution)/shard_map/ppermute | solution.py:211
  22.3 9.2 %collective-permute-start.3 = (f32[128,8,128]{2,1,0:T(8,128)S(1)}, f32[128,8,128]{2,1,0:T(8,128)S(1)}, u32[]{:S(2)}, u32[]{:S(2)}) collective-permute-start(f32[128,8,128]{2,1,0:T(8,128)S(1)} %get-tuple-element.219), channel_id=1, source_target_pairs={{0,4},{1,3},{2,6},{3,1},{4,0},{5,7},{6,2},{7,5},{8,12},{9,11},{10,... | collective-permute-start | bytes 1572872 | tf_op jit(solution)/shard_map/ppermute | solution.py:211
  25.2 7.9 %collective-permute-start.2 = (f32[256,8,128]{2,1,0:T(8,128)S(1)}, f32[256,8,128]{2,1,0:T(8,128)S(1)}, u32[]{:S(2)}, u32[]{:S(2)}) collective-permute-start(f32[256,8,128]{2,1,0:T(8,128)S(1)} %get-tuple-element.217), channel_id=1, source_target_pairs={{0,1},{1,0},{2,3},{3,2},{4,5},{5,4},{6,7},{7,6},{8,9},{9,8},{10,11... | collective-permute-start | bytes 3145736 | tf_op jit(solution)/shard_map/ppermute | solution.py:211
  28.7 14.1 %collective-permute-start.5 = (f32[304,8,128]{2,1,0:T(8,128)S(1)}, f32[304,8,128]{2,1,0:T(8,128)S(1)}, u32[]{:S(2)}, u32[]{:S(2)}) collective-permute-start(f32[304,8,128]{2,1,0:T(8,128)S(1)} %get-tuple-element.235), channel_id=1, source_target_pairs={{0,1},{1,0},{2,3},{3,2},{4,5},{5,4},{6,7},{7,6},{8,9},{9,8},{10,11... | collective-permute-start | bytes 3735560 | tf_op jit(solution)/shard_map/ppermute | solution.py:211
  31.6 9.2 %collective-permute-start.6 = (f32[64,8,128]{2,1,0:T(8,128)S(1)}, f32[64,8,128]{2,1,0:T(8,128)S(1)}, u32[]{:S(2)}, u32[]{:S(2)}) collective-permute-start(f32[64,8,128]{2,1,0:T(8,128)S(1)} %get-tuple-element.237), channel_id=1, source_target_pairs={{0,2},{1,5},{2,0},{3,7},{4,6},{5,1},{6,4},{7,3},{8,10},{9,13},{10,... | collective-permute-start | bytes 786440 | tf_op jit(solution)/shard_map/ppermute | solution.py:211
  33.2 11.9 %collective-permute-start.4 = (f32[128,8,128]{2,1,0:T(8,128)S(1)}, f32[128,8,128]{2,1,0:T(8,128)S(1)}, u32[]{:S(2)}, u32[]{:S(2)}) collective-permute-start(f32[128,8,128]{2,1,0:T(8,128)S(1)} %get-tuple-element.232), channel_id=1, source_target_pairs={{0,4},{1,3},{2,6},{3,1},{4,0},{5,7},{6,2},{7,5},{8,12},{9,11},{10,... | collective-permute-start | bytes 1572872 | tf_op jit(solution)/shard_map/ppermute | solution.py:211
  40.8 11.7 %collective-permute-start.8 = (f32[64,8,128]{2,1,0:T(8,128)S(1)}, f32[64,8,128]{2,1,0:T(8,128)S(1)}, u32[]{:S(2)}, u32[]{:S(2)}) collective-permute-start(f32[64,8,128]{2,1,0:T(8,128)S(1)} %get-tuple-element.248.refs_0_), channel_id=1, source_target_pairs={{0,8},{1,17},{2,10},{3,19},{4,12},{5,21},{6,14},{7,23},{8,0},{9,25... | collective-permute-start | bytes 786440 | tf_op jit(solution)/shard_map/ppermute | solution.py:211
  42.9 12.1 %collective-permute-start.7 = (f32[152,8,128]{2,1,0:T(8,128)S(1)}, f32[152,8,128]{2,1,0:T(8,128)S(1)}, u32[]{:S(2)}, u32[]{:S(2)}) collective-permute-start(f32[152,8,128]{2,1,0:T(8,128)S(1)} %get-tuple-element.247), channel_id=1, source_target_pairs={{0,4},{1,3},{2,6},{3,1},{4,0},{5,7},{6,2},{7,5},{8,12},{9,11},{10,... | collective-permute-start | bytes 1867784 | tf_op jit(solution)/shard_map/ppermute | solution.py:211
  45.2 13.6 %collective-permute-start.10 = (f32[64,8,128]{2,1,0:T(8,128)S(1)}, f32[64,8,128]{2,1,0:T(8,128)S(1)}, u32[]{:S(2)}, u32[]{:S(2)}) collective-permute-start(f32[64,8,128]{2,1,0:T(8,128)S(1)} %get-tuple-element.258), channel_id=1, source_target_pairs={{0,8},{1,17},{2,10},{3,19},{4,12},{5,21},{6,14},{7,23},{8,0},{9,25... | collective-permute-start | bytes 786440 | tf_op jit(solution)/shard_map/ppermute | solution.py:211
  52.5 13.2 %collective-permute-start.12 = (f32[64,8,128]{2,1,0:T(8,128)S(1)}, f32[64,8,128]{2,1,0:T(8,128)S(1)}, u32[]{:S(2)}, u32[]{:S(2)}) collective-permute-start(f32[64,8,128]{2,1,0:T(8,128)S(1)} %get-tuple-element.262.refs_0_), channel_id=1, source_target_pairs={{0,16},{1,9},{2,18},{3,11},{4,20},{5,13},{6,22},{7,15},{8,24},{9,1... | collective-permute-start | bytes 786440 | tf_op jit(solution)/shard_map/ppermute | solution.py:211
  58.8 7.4 %collective-permute-start.11 = (f32[32,8,128]{2,1,0:T(8,128)S(1)}, f32[32,8,128]{2,1,0:T(8,128)S(1)}, u32[]{:S(2)}, u32[]{:S(2)}) collective-permute-start(f32[32,8,128]{2,1,0:T(8,128)S(1)} %get-tuple-element.261), channel_id=1, source_target_pairs={{0,2},{1,5},{2,0},{3,7},{4,6},{5,1},{6,4},{7,3},{8,10},{9,13},{10,... | collective-permute-start | bytes 393224 | tf_op jit(solution)/shard_map/ppermute | solution.py:211
  65.8 9.5 %collective-permute-start.18 = (f32[64,8,128]{2,1,0:T(8,128)S(1)}, f32[64,8,128]{2,1,0:T(8,128)S(1)}, u32[]{:S(2)}, u32[]{:S(2)}) collective-permute-start(f32[64,8,128]{2,1,0:T(8,128)S(1)} %get-tuple-element.275.refs_0_), channel_id=1, source_target_pairs={{0,2},{1,5},{2,0},{3,7},{4,6},{5,1},{6,4},{7,3},{8,10},{9,13},{10,... | collective-permute-start | bytes 786440 | tf_op jit(solution)/shard_map/ppermute | solution.py:211
  66.3 7.3 %collective-permute-start.14 = (f32[32,8,128]{2,1,0:T(8,128)S(1)}, f32[32,8,128]{2,1,0:T(8,128)S(1)}, u32[]{:S(2)}, u32[]{:S(2)}) collective-permute-start(f32[32,8,128]{2,1,0:T(8,128)S(1)} %get-tuple-element.268.refs_0_), channel_id=1, source_target_pairs={{0,16},{1,9},{2,18},{3,11},{4,20},{5,13},{6,22},{7,15},{8,24},{9,1... | collective-permute-start | bytes 393224 | tf_op jit(solution)/shard_map/ppermute | solution.py:211
  69.0 8.0 %collective-permute-start.17 = (f32[38,8,128]{2,1,0:T(8,128)S(1)}, f32[38,8,128]{2,1,0:T(8,128)S(1)}, u32[]{:S(2)}, u32[]{:S(2)}) collective-permute-start(f32[38,8,128]{2,1,0:T(8,128)S(1)} %get-tuple-element.274.refs_0_), channel_id=1, source_target_pairs={{0,16},{1,9},{2,18},{3,11},{4,20},{5,13},{6,22},{7,15},{8,24},{9,1... | collective-permute-start | bytes 466952 | tf_op jit(solution)/shard_map/ppermute | solution.py:211
  69.4 11.2 %collective-permute-start.9 = (f32[72,512]{1,0:T(8,128)S(1)}, f32[72,512]{1,0:T(8,128)S(1)}, u32[]{:S(2)}, u32[]{:S(2)}) collective-permute-start(f32[72,512]{1,0:T(8,128)S(1)} %get-tuple-element.254), channel_id=1, source_target_pairs={{1,0},{2,1},{3,2},{4,3},{5,4},{6,5},{7,6},{8,7},{9,8},{10,9},{11,1... | collective-permute-start | bytes 442376 | tf_op jit(solution)/shard_map/ppermute | solution.py:582
  75.4 17.0 %collective-permute-start.30 = (f32[128,8,128]{2,1,0:T(8,128)S(1)}, f32[128,8,128]{2,1,0:T(8,128)S(1)}, u32[]{:S(2)}, u32[]{:S(2)}) collective-permute-start(f32[128,8,128]{2,1,0:T(8,128)S(1)} %get-tuple-element.290.refs_5_), channel_id=1, source_target_pairs={{0,1},{1,0},{2,3},{3,2},{4,5},{5,4},{6,7},{7,6},{8,9},{9,8},{10,11... | collective-permute-start | bytes 1572872 | tf_op jit(solution)/shard_map/ppermute | solution.py:211
  75.4 16.3 %collective-permute-start.28 = (f32[128,8,128]{2,1,0:T(8,128)S(1)}, f32[128,8,128]{2,1,0:T(8,128)S(1)}, u32[]{:S(2)}, u32[]{:S(2)}) collective-permute-start(f32[128,8,128]{2,1,0:T(8,128)S(1)} %get-tuple-element.290.refs_5_), channel_id=1, source_target_pairs={{0,4},{1,3},{2,6},{3,1},{4,0},{5,7},{6,2},{7,5},{8,12},{9,11},{10,... | collective-permute-start | bytes 1572872 | tf_op jit(solution)/shard_map/ppermute | solution.py:211
  80.0 8.7 %collective-permute-start.21 = (f32[64,8,128]{2,1,0:T(8,128)S(1)}, f32[64,8,128]{2,1,0:T(8,128)S(1)}, u32[]{:S(2)}, u32[]{:S(2)}) collective-permute-start(f32[64,8,128]{2,1,0:T(8,128)S(1)} %get-tuple-element.285.refs_0_), channel_id=1, source_target_pairs={{0,8},{1,17},{2,10},{3,19},{4,12},{5,21},{6,14},{7,23},{8,0},{9,25... | collective-permute-start | bytes 786440 | tf_op jit(solution)/shard_map/ppermute | solution.py:211
  84.1 8.2 %collective-permute-start.20 = (f32[76,8,128]{2,1,0:T(8,128)S(1)}, f32[76,8,128]{2,1,0:T(8,128)S(1)}, u32[]{:S(2)}, u32[]{:S(2)}) collective-permute-start(f32[76,8,128]{2,1,0:T(8,128)S(1)} %get-tuple-element.284.refs_0_), channel_id=1, source_target_pairs={{0,2},{1,5},{2,0},{3,7},{4,6},{5,1},{6,4},{7,3},{8,10},{9,13},{10,... | collective-permute-start | bytes 933896 | tf_op jit(solution)/shard_map/ppermute | solution.py:211
  88.7 10.2 %collective-permute-start.24 = (f32[128,8,128]{2,1,0:T(8,128)S(1)}, f32[128,8,128]{2,1,0:T(8,128)S(1)}, u32[]{:S(2)}, u32[]{:S(2)}) collective-permute-start(f32[128,8,128]{2,1,0:T(8,128)S(1)} %get-tuple-element.289.refs_0_), channel_id=1, source_target_pairs={{0,4},{1,3},{2,6},{3,1},{4,0},{5,7},{6,2},{7,5},{8,12},{9,11},{10,... | collective-permute-start | bytes 1572872 | tf_op jit(solution)/shard_map/ppermute | solution.py:211
  91.7 7.2 %collective-permute-start.27 = (f32[128,8,128]{2,1,0:T(8,128)S(1)}, f32[128,8,128]{2,1,0:T(8,128)S(1)}, u32[]{:S(2)}, u32[]{:S(2)}) collective-permute-start(f32[128,8,128]{2,1,0:T(8,128)S(1)} %get-tuple-element.289.refs_0_), channel_id=1, source_target_pairs={{0,1},{1,0},{2,3},{3,2},{4,5},{5,4},{6,7},{7,6},{8,9},{9,8},{10,11... | collective-permute-start | bytes 1572872 | tf_op jit(solution)/shard_map/ppermute | solution.py:211
  91.7 7.2 %collective-permute-start.29 = (f32[128,8,128]{2,1,0:T(8,128)S(1)}, f32[128,8,128]{2,1,0:T(8,128)S(1)}, u32[]{:S(2)}, u32[]{:S(2)}) collective-permute-start(f32[128,8,128]{2,1,0:T(8,128)S(1)} %collective-permute-done.28.refs_6_), channel_id=1, source_target_pairs={{0,1},{1,0},{2,3},{3,2},{4,5},{5,4},{6,7},{7,6},{8,9},{9,8},{10,11... | collective-permute-start | bytes 1572872 | tf_op jit(solution)/shard_map/ppermute | solution.py:211
  92.3 13.3 %collective-permute-start.26 = (f32[152,8,128]{2,1,0:T(8,128)S(1)}, f32[152,8,128]{2,1,0:T(8,128)S(1)}, u32[]{:S(2)}, u32[]{:S(2)}) collective-permute-start(f32[152,8,128]{2,1,0:T(8,128)S(1)} %get-tuple-element.288.refs_0_.refs_8_), channel_id=1, source_target_pairs={{0,1},{1,0},{2,3},{3,2},{4,5},{5,4},{6,7},{7,6},{8,9},{9,8},{10,11... | collective-permute-start | bytes 1867784 | tf_op jit(solution)/shard_map/ppermute | solution.py:211
  92.4 13.2 %collective-permute-start.22 = (f32[152,8,128]{2,1,0:T(8,128)S(1)}, f32[152,8,128]{2,1,0:T(8,128)S(1)}, u32[]{:S(2)}, u32[]{:S(2)}) collective-permute-start(f32[152,8,128]{2,1,0:T(8,128)S(1)} %get-tuple-element.288.refs_0_.refs_8_), channel_id=1, source_target_pairs={{0,4},{1,3},{2,6},{3,1},{4,0},{5,7},{6,2},{7,5},{8,12},{9,11},{10,... | collective-permute-start | bytes 1867784 | tf_op jit(solution)/shard_map/ppermute | solution.py:211
  (25 other events, 133.8 us)

commit v3 on v2

--- a/solution.py
+++ b/solution.py
@@ -788,7 +788,7 @@
             [few_update()] if "f" in word else []
         )
 
-    for word in SCRIPT.split():
+    for word in SCRIPT:
         if word in owners:
             sums[word].advance()
         elif word == "gg":
@@ -809,10 +809,11 @@
 
 
 WHOLE = (2, 1, 1)
-SCRIPT = """
-jP gg kP P j0 k0 j1 k1 P 0 sg0 P 1 back 0 mix0 P 1 mix1 0 1 P 0 1 0 P 1 0 sP rP sg1 1 0 s0 1 s1 =Pb r0 =0abPacd
-r1 =1a =0cd1bc =1df
-"""
+SCRIPT = (
+    "jP", "gg", "kP", "P", "j0", "k0", "j1", "k1", "P", "0", "sg0", "P", "1", "back", "0", "mix0",
+    "P", "1", "mix1", "0", "1", "P", "0", "1", "0", "P", "1", "0", "sP", "rP", "sg1", "1", "0",
+    "s0", "1", "s1", "=Pb", "r0", "=0abPacd", "r1", "=1a", "=0cd1bc", "=1df",
+)
 
 
 def shards(*args):

time: 112 us -> 112 us (level)
  no operation moved by 1% of the time
where the time goes in v3:
time: 112 us
  Pallas kernels  47.9 us (43%)
  starting transfers between devices  34.3 us (31%)
  waiting for transfers between devices  28 us (25%)
  between operations  1.42 us (1%)
    pallas_call x40, Pallas kernels, call(): pl.pallas_call(run, out_shape=[kinds[id(s)](*o) for o, s in zip(outs, out...  47.9 us
    ppermute x29, starting transfers between devices, swap(): return lax.ppermute(x, axes, self.pairs[step])  30.2 us
    ppermute x29, waiting for transfers between devices, swap(): return lax.ppermute(x, axes, self.pairs[step])  28 us
    ppermute x1, starting transfers between devices, solve(): halo = lax.ppermute(packed, axes, [(i, i + 1) for i in range(count - 1)])  2.63 us
  transfers between devices with their start and end apart: 31, of which 13 were waited for; matrix products, arithmetic and copies ran while one was open for 0% of the time, Pallas kernels for 34%

profile of v3, /device:TPU:0, one launch (start us, length us, event | category | flops | bytes accessed | tf_op | source)
XLA Modules:
  0.0 111.7 jit_solution(944382072210068072)
XLA Ops:
  1.8 2.6 %collective-permute-start = (f32[72,512]{1,0:T(8,128)S(1)}, f32[72,512]{1,0:T(8,128)S(1)}, u32[]{:S(2)}, u32[]{:S(2)}) collective-permute-start(f32[72,512]{1,0:T(8,128)S(1)} %get-tuple-element.178), channel_id=1, source_target_pairs={{0,1},{1,2},{2,3},{3,4},{4,5},{5,6},{6,7},{7,8},{8,9},{9,10},{10,1... | collective-permute-start | bytes 442376 | tf_op jit(solution)/shard_map/ppermute | solution.py:445
  4.6 4.3 %late_gates.1 = (bf16[512,512]{1,0:T(8,128)(2,1)S(1)}, f8e5m2[512,512]{1,0:T(32,128)(4,1)S(1)}, f8e5m2[512,512]{1,0:T(32,128)(4,1)S(1)}, bf16[512,512]{1,0:T(8,1...) custom-call(f32[1024,512]{1,0:T(8,128)S(1)} %copy-done.10, ...), custom_call_target="tpu_custom_call" | custom-call | flops 11600000000 | bytes 1 | tf_op jit(solution)/shard_map/late_gates/pallas_call | solution.py:72
  8.9 4.4 %early_gates.1 = (bf16[512,512]{1,0:T(8,128)(2,1)S(1)}, f8e5m2[512,512]{1,0:T(32,128)(4,1)S(1)}, f8e5m2[512,512]{1,0:T(32,128)(4,1)S(1)}, bf16[512,128]{1,0:T(8,...) custom-call(f32[72,512]{1,0:T(8,128)S(1)} %collective-permute-done.r, ...), custom_call_target="tpu_custom_call" | custom-call | flops 12760000512 | bytes 1 | tf_op jit(solution)/shard_map/early_gates/pallas_call | solution.py:72
  14.6 2.7 %collective-permute-start.1 = (f32[256,8,128]{2,1,0:T(8,128)S(1)}, f32[256,8,128]{2,1,0:T(8,128)S(1)}, u32[]{:S(2)}, u32[]{:S(2)}) collective-permute-start(f32[256,8,128]{2,1,0:T(8,128)S(1)} %get-tuple-element.212), channel_id=1, source_target_pairs={{0,1},{1,0},{2,3},{3,2},{4,5},{5,4},{6,7},{7,6},{8,9},{9,8},{10,11... | collective-permute-start | bytes 3145736 | tf_op jit(solution)/shard_map/ppermute | solution.py:211
  17.3 3.3 %gate_grad.1 = (bf16[1024,1024]{1,0:T(8,128)(2,1)S(1)}, f8e5m2[1024,1024]{1,0:T(32,128)(4,1)S(1)}, f8e5m2[1024,1024]{1,0:T(32,128)(4,1)S(1)}, f32[8,128]{1,0:T(8,128)S(1)}) custom-call(bf16[1024,1024]{1,0:T(8,128)(2,1)S(1)} %get-tuple-element.198.refs_6_.refs_0_, f8e4m3fn[1024,1024]{1,0:T(32,128)(4,1)S(1)} %get-tuple-element.199.refs_7_.refs_1_, ...), custom_call_target="tpu_custom_call" | custom-call | flops 9859999744 | bytes 1 | tf_op jit(solution)/shard_map/gate_grad/pallas_call | solution.py:72
  26.6 2.0 %tap1_grad0.1 = (f32[304,8,128]{2,1,0:T(8,128)S(1)}, f32[4,24,8,128]{3,2,1,0:T(8,128)S(1)}, f32[16,1024]{1,0:T(8,128)S(1)}, f32[8,128]{1,0:T(8,128)S(1)}) custom-call(bf16[512,512]{1,0:T(8,128)(2,1)S(1)} %get-tuple-element.179.refs_2_.refs_0_, f8e5m2[512,512]{1,0:T(32,128)(4,1)S(1)} %get-tuple-element.180.refs_3_.refs_1_, ...), custom_call_target="tpu_custom_call" | custom-call | flops 5800000000 | bytes 1 | tf_op jit(solution)/shard_map/tap1_grad0/pallas_call | solution.py:72
  34.8 3.5 %do_sg.2 = (f32[1024,512]{1,0:T(8,128)}, f32[8,128]{1,0:T(8,128)S(1)}) custom-call(bf16[1024,1024]{1,0:T(8,128)(2,1)S(1)} %get-tuple-element.207.refs_6_.refs_0_, f8e5m2[1024,1024]{1,0:T(32,128)(4,1)S(1)} %get-tuple-element.208.refs_7_.refs_1_, f8e5m2[1024,1024]{1,0:T(32,128)(4,1)S(1)} %get-tuple-element.209.refs_8_.refs_2_, ...), custom_call_target="tpu_custom_call" | custom-call | flops 10149999616 | bytes 1 | tf_op jit(solution)/shard_map/do_sg/pallas_call | solution.py:72
  38.3 2.4 %collective-permute-done.6.refs_1_ = f32[64,8,128]{2,1,0:T(8,128)S(1)} collective-permute-done((f32[64,8,128]{2,1,0:T(8,128)S(1)}, f32[64,8,128]{2,1,0:T(8,128)S(1)}, u32[]{:S(2)}, u32[]{:S(2)}) %collective-permute-start.6) | collective-permute-done | bytes 262176 | tf_op jit(solution)/shard_map/ppermute | solution.py:211
  45.8 2.2 %do_mix.2 = (f32[1024,512]{1,0:T(8,128)}, f32[1024,512]{1,0:T(8,128)}, f32[8,128]{1,0:T(8,128)S(1)}) custom-call(bf16[512,512]{1,0:T(8,128)(2,1)S(1)} %get-tuple-element.189.refs_0_, f8e4m3fn[512,512]{1,0:T(32,128)(4,1)S(1)} %get-tuple-element.190.refs_1_, f8e4m3fn[512,512]{1,0:T(32,128)(4,1)S(1)} %get-tuple-element.191.refs_2_, ...), custom_call_target="tpu_custom_call" | custom-call | flops 6380000256 | bytes 1 | tf_op jit(solution)/shard_map/do_mix/pallas_call | solution.py:72
  48.0 4.4 %collective-permute-done.8.refs_1_ = f32[64,8,128]{2,1,0:T(8,128)S(1)} collective-permute-done((f32[64,8,128]{2,1,0:T(8,128)S(1)}, f32[64,8,128]{2,1,0:T(8,128)S(1)}, u32[]{:S(2)}, u32[]{:S(2)}) %collective-permute-start.8) | collective-permute-done | bytes 262176 | tf_op jit(solution)/shard_map/ppermute | solution.py:211
  52.5 2.5 %collective-permute-start.12 = (f32[64,8,128]{2,1,0:T(8,128)S(1)}, f32[64,8,128]{2,1,0:T(8,128)S(1)}, u32[]{:S(2)}, u32[]{:S(2)}) collective-permute-start(f32[64,8,128]{2,1,0:T(8,128)S(1)} %get-tuple-element.262.refs_0_), channel_id=1, source_target_pairs={{0,16},{1,9},{2,18},{3,11},{4,20},{5,13},{6,22},{7,15},{8,24},{9,1... | collective-permute-start | bytes 786440 | tf_op jit(solution)/shard_map/ppermute | solution.py:211
  55.9 2.2 %do_mix.3 = (f32[1024,512]{1,0:T(8,128)}, f32[1024,512]{1,0:T(8,128)}, f32[8,128]{1,0:T(8,128)S(1)}) custom-call(bf16[512,512]{1,0:T(8,128)(2,1)S(1)} %get-tuple-element.175.refs_3_.refs_0_, f8e4m3fn[512,512]{1,0:T(32,128)(4,1)S(1)} %get-tuple-element.176.refs_4_.refs_1_, ...), custom_call_target="tpu_custom_call", output_to_operand_aliasing={{0}: (8, {}), {1}: (9, {})} | custom-call | flops 6380000256 | bytes 1 | tf_op jit(solution)/shard_map/do_mix/pallas_call | solution.py:72
  62.0 2.5 %collective-permute-start.15 = (f32[38,8,128]{2,1,0:T(8,128)S(1)}, f32[38,8,128]{2,1,0:T(8,128)S(1)}, u32[]{:S(2)}, u32[]{:S(2)}) collective-permute-start(f32[38,8,128]{2,1,0:T(8,128)S(1)} %get-tuple-element.270), channel_id=1, source_target_pairs={{0,8},{1,17},{2,10},{3,19},{4,12},{5,21},{6,14},{7,23},{8,0},{9,25... | collective-permute-start | bytes 466952 | tf_op jit(solution)/shard_map/ppermute | solution.py:211
  66.3 2.6 %collective-permute-done.15.refs_1_ = f32[38,8,128]{2,1,0:T(8,128)S(1)} collective-permute-done((f32[38,8,128]{2,1,0:T(8,128)S(1)}, f32[38,8,128]{2,1,0:T(8,128)S(1)}, u32[]{:S(2)}, u32[]{:S(2)}) %collective-permute-start.15) | collective-permute-done | bytes 155680 | tf_op jit(solution)/shard_map/ppermute | solution.py:211
  70.9 2.7 %collective-permute-done.14.refs_1_ = f32[32,8,128]{2,1,0:T(8,128)S(1)} collective-permute-done((f32[32,8,128]{2,1,0:T(8,128)S(1)}, f32[32,8,128]{2,1,0:T(8,128)S(1)}, u32[]{:S(2)}, u32[]{:S(2)}) %collective-permute-start.14) | collective-permute-done | bytes 131104 | tf_op jit(solution)/shard_map/ppermute | solution.py:211
  77.3 2.6 %collective-permute-done.16.refs_1_ = f32[32,8,128]{2,1,0:T(8,128)S(1)} collective-permute-done((f32[32,8,128]{2,1,0:T(8,128)S(1)}, f32[32,8,128]{2,1,0:T(8,128)S(1)}, u32[]{:S(2)}, u32[]{:S(2)}) %collective-permute-start.16) | collective-permute-done | bytes 131104 | tf_op jit(solution)/shard_map/ppermute | solution.py:211
  80.5 3.5 %do_sg.3 = (f32[1024,512]{1,0:T(8,128)}, f32[7,80]{1,0:T(8,128)}, f32[8,128]{1,0:T(8,128)S(1)}) custom-call(bf16[1024,1024]{1,0:T(8,128)(2,1)S(1)} %get-tuple-element.207.refs_6_.refs_0_, f8e5m2[1024,1024]{1,0:T(32,128)(4,1)S(1)} %get-tuple-element.208.refs_7_.refs_1_, ...), custom_call_target="tpu_custom_call", output_to_operand_aliasing={{0}: (10, {})} | custom-call | flops 10149999616 | bytes 1 | tf_op jit(solution)/shard_map/do_sg/pallas_call | solution.py:72
  84.1 2.2 %collective-permute-start.20 = (f32[76,8,128]{2,1,0:T(8,128)S(1)}, f32[76,8,128]{2,1,0:T(8,128)S(1)}, u32[]{:S(2)}, u32[]{:S(2)}) collective-permute-start(f32[76,8,128]{2,1,0:T(8,128)S(1)} %get-tuple-element.284.refs_0_), channel_id=1, source_target_pairs={{0,2},{1,5},{2,0},{3,7},{4,6},{5,1},{6,4},{7,3},{8,10},{9,13},{10,... | collective-permute-start | bytes 933896 | tf_op jit(solution)/shard_map/ppermute | solution.py:211
  86.2 2.4 %collective-permute-done.21.refs_1_ = f32[64,8,128]{2,1,0:T(8,128)S(1)} collective-permute-done((f32[64,8,128]{2,1,0:T(8,128)S(1)}, f32[64,8,128]{2,1,0:T(8,128)S(1)}, u32[]{:S(2)}, u32[]{:S(2)}) %collective-permute-start.21) | collective-permute-done | bytes 262176 | tf_op jit(solution)/shard_map/ppermute | solution.py:211
  88.7 3.0 %collective-permute-start.24 = (f32[128,8,128]{2,1,0:T(8,128)S(1)}, f32[128,8,128]{2,1,0:T(8,128)S(1)}, u32[]{:S(2)}, u32[]{:S(2)}) collective-permute-start(f32[128,8,128]{2,1,0:T(8,128)S(1)} %get-tuple-element.289.refs_0_), channel_id=1, source_target_pairs={{0,4},{1,3},{2,6},{3,1},{4,0},{5,7},{6,2},{7,5},{8,12},{9,11},{10,... | collective-permute-start | bytes 1572872 | tf_op jit(solution)/shard_map/ppermute | solution.py:211
  95.0 3.9 %collective-permute-done.24.refs_0_ = f32[128,8,128]{2,1,0:T(8,128)S(1)} collective-permute-done((f32[128,8,128]{2,1,0:T(8,128)S(1)}, f32[128,8,128]{2,1,0:T(8,128)S(1)}, u32[]{:S(2)}, u32[]{:S(2)}) %collective-permute-start.24) | collective-permute-done | bytes 524320 | tf_op jit(solution)/shard_map/ppermute | solution.py:211
  98.9 3.9 %do_u2_u3.1 = (f32[2,512,1024]{2,1,0:T(8,128)}, f32[2,512,1024]{2,1,0:T(8,128)}, f32[2,512,1024]{2,1,0:T(8,128)}, bf16[2,512,1024]{2,1,0:T(8,128)(2,1)}, f32[512...) custom-call(f32[128,8,128]{2,1,0:T(8,128)S(1)} %get-tuple-element.28, ...), custom_call_target="tpu_custom_call", output_to_operand_aliasing={{4}: (11, {}), {5}: (12, {}), {6}: (13, {}), {7}: (14, {})} | custom-call | flops 11310000128 | bytes 1 | tf_op jit(solution)/shard_map/do_u2_u3/pallas_call | solution.py:72
  105.6 3.3 %do_u4.1 = (f32[2,512,1024]{2,1,0:T(8,128)}, f32[2,512,1024]{2,1,0:T(8,128)}, f32[2,512,1024]{2,1,0:T(8,128)}, bf16[2,512,1024]{2,1,0:T(8,128)(2,1)}, f32[8,128]{1,0:T(8,128)S(1)}) custom-call(f32[128,8,128]{2,1,0:T(8,128)S(1)} %collective-permute-done.24.refs_0_, ...), custom_call_target="tpu_custom_call", output_to_operand_aliasing={{0}: (7, {}), {1}: (8, {}), {2}: (9, {}), {3}: (10, {})} | custom-call | flops 9280000000 | bytes 1 | tf_op jit(solution)/shard_map/do_u4/pallas_call | solution.py:72
  108.9 2.6 %do_u1_few.1 = (f32[2,512,1024]{2,1,0:T(8,128)}, f32[2,512,1024]{2,1,0:T(8,128)}, f32[2,512,1024]{2,1,0:T(8,128)}, bf16[2,512,1024]{2,1,0:T(8,128)(2,1)}, f32[80...) custom-call(f32[152,8,128]{2,1,0:T(8,128)S(1)} %collective-permute-d, ...), custom_call_target="tpu_custom_call", output_to_operand_aliasing={{0}: (4, {}), {1}: (5, {}), {2}: (6, {}), {3}: (7, {})} | custom-call | flops 6380000256 | bytes 1 | tf_op jit(solution)/shard_map/do_u1_few/pallas_call | solution.py:72
  (114 shorter events, 38.5 us)
Async XLA Ops:
  14.6 7.5 %collective-permute-start.1 = (f32[256,8,128]{2,1,0:T(8,128)S(1)}, f32[256,8,128]{2,1,0:T(8,128)S(1)}, u32[]{:S(2)}, u32[]{:S(2)}) collective-permute-start(f32[256,8,128]{2,1,0:T(8,128)S(1)} %get-tuple-element.212), channel_id=1, source_target_pairs={{0,1},{1,0},{2,3},{3,2},{4,5},{5,4},{6,7},{7,6},{8,9},{9,8},{10,11... | collective-permute-start | bytes 3145736 | tf_op jit(solution)/shard_map/ppermute | solution.py:211
  22.3 9.2 %collective-permute-start.3 = (f32[128,8,128]{2,1,0:T(8,128)S(1)}, f32[128,8,128]{2,1,0:T(8,128)S(1)}, u32[]{:S(2)}, u32[]{:S(2)}) collective-permute-start(f32[128,8,128]{2,1,0:T(8,128)S(1)} %get-tuple-element.219), channel_id=1, source_target_pairs={{0,4},{1,3},{2,6},{3,1},{4,0},{5,7},{6,2},{7,5},{8,12},{9,11},{10,... | collective-permute-start | bytes 1572872 | tf_op jit(solution)/shard_map/ppermute | solution.py:211
  25.2 7.9 %collective-permute-start.2 = (f32[256,8,128]{2,1,0:T(8,128)S(1)}, f32[256,8,128]{2,1,0:T(8,128)S(1)}, u32[]{:S(2)}, u32[]{:S(2)}) collective-permute-start(f32[256,8,128]{2,1,0:T(8,128)S(1)} %get-tuple-element.217), channel_id=1, source_target_pairs={{0,1},{1,0},{2,3},{3,2},{4,5},{5,4},{6,7},{7,6},{8,9},{9,8},{10,11... | collective-permute-start | bytes 3145736 | tf_op jit(solution)/shard_map/ppermute | solution.py:211
  28.7 14.1 %collective-permute-start.5 = (f32[304,8,128]{2,1,0:T(8,128)S(1)}, f32[304,8,128]{2,1,0:T(8,128)S(1)}, u32[]{:S(2)}, u32[]{:S(2)}) collective-permute-start(f32[304,8,128]{2,1,0:T(8,128)S(1)} %get-tuple-element.235), channel_id=1, source_target_pairs={{0,1},{1,0},{2,3},{3,2},{4,5},{5,4},{6,7},{7,6},{8,9},{9,8},{10,11... | collective-permute-start | bytes 3735560 | tf_op jit(solution)/shard_map/ppermute | solution.py:211
  31.6 9.2 %collective-permute-start.6 = (f32[64,8,128]{2,1,0:T(8,128)S(1)}, f32[64,8,128]{2,1,0:T(8,128)S(1)}, u32[]{:S(2)}, u32[]{:S(2)}) collective-permute-start(f32[64,8,128]{2,1,0:T(8,128)S(1)} %get-tuple-element.237), channel_id=1, source_target_pairs={{0,2},{1,5},{2,0},{3,7},{4,6},{5,1},{6,4},{7,3},{8,10},{9,13},{10,... | collective-permute-start | bytes 786440 | tf_op jit(solution)/shard_map/ppermute | solution.py:211
  33.2 11.9 %collective-permute-start.4 = (f32[128,8,128]{2,1,0:T(8,128)S(1)}, f32[128,8,128]{2,1,0:T(8,128)S(1)}, u32[]{:S(2)}, u32[]{:S(2)}) collective-permute-start(f32[128,8,128]{2,1,0:T(8,128)S(1)} %get-tuple-element.232), channel_id=1, source_target_pairs={{0,4},{1,3},{2,6},{3,1},{4,0},{5,7},{6,2},{7,5},{8,12},{9,11},{10,... | collective-permute-start | bytes 1572872 | tf_op jit(solution)/shard_map/ppermute | solution.py:211
  40.8 11.7 %collective-permute-start.8 = (f32[64,8,128]{2,1,0:T(8,128)S(1)}, f32[64,8,128]{2,1,0:T(8,128)S(1)}, u32[]{:S(2)}, u32[]{:S(2)}) collective-permute-start(f32[64,8,128]{2,1,0:T(8,128)S(1)} %get-tuple-element.248.refs_0_), channel_id=1, source_target_pairs={{0,8},{1,17},{2,10},{3,19},{4,12},{5,21},{6,14},{7,23},{8,0},{9,25... | collective-permute-start | bytes 786440 | tf_op jit(solution)/shard_map/ppermute | solution.py:211
  42.9 12.1 %collective-permute-start.7 = (f32[152,8,128]{2,1,0:T(8,128)S(1)}, f32[152,8,128]{2,1,0:T(8,128)S(1)}, u32[]{:S(2)}, u32[]{:S(2)}) collective-permute-start(f32[152,8,128]{2,1,0:T(8,128)S(1)} %get-tuple-element.247), channel_id=1, source_target_pairs={{0,4},{1,3},{2,6},{3,1},{4,0},{5,7},{6,2},{7,5},{8,12},{9,11},{10,... | collective-permute-start | bytes 1867784 | tf_op jit(solution)/shard_map/ppermute | solution.py:211
  45.2 13.6 %collective-permute-start.10 = (f32[64,8,128]{2,1,0:T(8,128)S(1)}, f32[64,8,128]{2,1,0:T(8,128)S(1)}, u32[]{:S(2)}, u32[]{:S(2)}) collective-permute-start(f32[64,8,128]{2,1,0:T(8,128)S(1)} %get-tuple-element.258), channel_id=1, source_target_pairs={{0,8},{1,17},{2,10},{3,19},{4,12},{5,21},{6,14},{7,23},{8,0},{9,25... | collective-permute-start | bytes 786440 | tf_op jit(solution)/shard_map/ppermute | solution.py:211
  52.5 13.2 %collective-permute-start.12 = (f32[64,8,128]{2,1,0:T(8,128)S(1)}, f32[64,8,128]{2,1,0:T(8,128)S(1)}, u32[]{:S(2)}, u32[]{:S(2)}) collective-permute-start(f32[64,8,128]{2,1,0:T(8,128)S(1)} %get-tuple-element.262.refs_0_), channel_id=1, source_target_pairs={{0,16},{1,9},{2,18},{3,11},{4,20},{5,13},{6,22},{7,15},{8,24},{9,1... | collective-permute-start | bytes 786440 | tf_op jit(solution)/shard_map/ppermute | solution.py:211
  58.8 7.4 %collective-permute-start.11 = (f32[32,8,128]{2,1,0:T(8,128)S(1)}, f32[32,8,128]{2,1,0:T(8,128)S(1)}, u32[]{:S(2)}, u32[]{:S(2)}) collective-permute-start(f32[32,8,128]{2,1,0:T(8,128)S(1)} %get-tuple-element.261), channel_id=1, source_target_pairs={{0,2},{1,5},{2,0},{3,7},{4,6},{5,1},{6,4},{7,3},{8,10},{9,13},{10,... | collective-permute-start | bytes 393224 | tf_op jit(solution)/shard_map/ppermute | solution.py:211
  65.8 9.5 %collective-permute-start.18 = (f32[64,8,128]{2,1,0:T(8,128)S(1)}, f32[64,8,128]{2,1,0:T(8,128)S(1)}, u32[]{:S(2)}, u32[]{:S(2)}) collective-permute-start(f32[64,8,128]{2,1,0:T(8,128)S(1)} %get-tuple-element.275.refs_0_), channel_id=1, source_target_pairs={{0,2},{1,5},{2,0},{3,7},{4,6},{5,1},{6,4},{7,3},{8,10},{9,13},{10,... | collective-permute-start | bytes 786440 | tf_op jit(solution)/shard_map/ppermute | solution.py:211
  66.3 7.3 %collective-permute-start.14 = (f32[32,8,128]{2,1,0:T(8,128)S(1)}, f32[32,8,128]{2,1,0:T(8,128)S(1)}, u32[]{:S(2)}, u32[]{:S(2)}) collective-permute-start(f32[32,8,128]{2,1,0:T(8,128)S(1)} %get-tuple-element.268.refs_0_), channel_id=1, source_target_pairs={{0,16},{1,9},{2,18},{3,11},{4,20},{5,13},{6,22},{7,15},{8,24},{9,1... | collective-permute-start | bytes 393224 | tf_op jit(solution)/shard_map/ppermute | solution.py:211
  69.0 8.0 %collective-permute-start.17 = (f32[38,8,128]{2,1,0:T(8,128)S(1)}, f32[38,8,128]{2,1,0:T(8,128)S(1)}, u32[]{:S(2)}, u32[]{:S(2)}) collective-permute-start(f32[38,8,128]{2,1,0:T(8,128)S(1)} %get-tuple-element.274.refs_0_), channel_id=1, source_target_pairs={{0,16},{1,9},{2,18},{3,11},{4,20},{5,13},{6,22},{7,15},{8,24},{9,1... | collective-permute-start | bytes 466952 | tf_op jit(solution)/shard_map/ppermute | solution.py:211
  69.4 11.2 %collective-permute-start.9 = (f32[72,512]{1,0:T(8,128)S(1)}, f32[72,512]{1,0:T(8,128)S(1)}, u32[]{:S(2)}, u32[]{:S(2)}) collective-permute-start(f32[72,512]{1,0:T(8,128)S(1)} %get-tuple-element.254), channel_id=1, source_target_pairs={{1,0},{2,1},{3,2},{4,3},{5,4},{6,5},{7,6},{8,7},{9,8},{10,9},{11,1... | collective-permute-start | bytes 442376 | tf_op jit(solution)/shard_map/ppermute | solution.py:582
  75.4 17.0 %collective-permute-start.30 = (f32[128,8,128]{2,1,0:T(8,128)S(1)}, f32[128,8,128]{2,1,0:T(8,128)S(1)}, u32[]{:S(2)}, u32[]{:S(2)}) collective-permute-start(f32[128,8,128]{2,1,0:T(8,128)S(1)} %get-tuple-element.290.refs_5_), channel_id=1, source_target_pairs={{0,1},{1,0},{2,3},{3,2},{4,5},{5,4},{6,7},{7,6},{8,9},{9,8},{10,11... | collective-permute-start | bytes 1572872 | tf_op jit(solution)/shard_map/ppermute | solution.py:211
  75.4 16.3 %collective-permute-start.28 = (f32[128,8,128]{2,1,0:T(8,128)S(1)}, f32[128,8,128]{2,1,0:T(8,128)S(1)}, u32[]{:S(2)}, u32[]{:S(2)}) collective-permute-start(f32[128,8,128]{2,1,0:T(8,128)S(1)} %get-tuple-element.290.refs_5_), channel_id=1, source_target_pairs={{0,4},{1,3},{2,6},{3,1},{4,0},{5,7},{6,2},{7,5},{8,12},{9,11},{10,... | collective-permute-start | bytes 1572872 | tf_op jit(solution)/shard_map/ppermute | solution.py:211
  80.0 8.7 %collective-permute-start.21 = (f32[64,8,128]{2,1,0:T(8,128)S(1)}, f32[64,8,128]{2,1,0:T(8,128)S(1)}, u32[]{:S(2)}, u32[]{:S(2)}) collective-permute-start(f32[64,8,128]{2,1,0:T(8,128)S(1)} %get-tuple-element.285.refs_0_), channel_id=1, source_target_pairs={{0,8},{1,17},{2,10},{3,19},{4,12},{5,21},{6,14},{7,23},{8,0},{9,25... | collective-permute-start | bytes 786440 | tf_op jit(solution)/shard_map/ppermute | solution.py:211
  84.1 8.2 %collective-permute-start.20 = (f32[76,8,128]{2,1,0:T(8,128)S(1)}, f32[76,8,128]{2,1,0:T(8,128)S(1)}, u32[]{:S(2)}, u32[]{:S(2)}) collective-permute-start(f32[76,8,128]{2,1,0:T(8,128)S(1)} %get-tuple-element.284.refs_0_), channel_id=1, source_target_pairs={{0,2},{1,5},{2,0},{3,7},{4,6},{5,1},{6,4},{7,3},{8,10},{9,13},{10,... | collective-permute-start | bytes 933896 | tf_op jit(solution)/shard_map/ppermute | solution.py:211
  88.7 10.2 %collective-permute-start.24 = (f32[128,8,128]{2,1,0:T(8,128)S(1)}, f32[128,8,128]{2,1,0:T(8,128)S(1)}, u32[]{:S(2)}, u32[]{:S(2)}) collective-permute-start(f32[128,8,128]{2,1,0:T(8,128)S(1)} %get-tuple-element.289.refs_0_), channel_id=1, source_target_pairs={{0,4},{1,3},{2,6},{3,1},{4,0},{5,7},{6,2},{7,5},{8,12},{9,11},{10,... | collective-permute-start | bytes 1572872 | tf_op jit(solution)/shard_map/ppermute | solution.py:211
  91.7 7.2 %collective-permute-start.27 = (f32[128,8,128]{2,1,0:T(8,128)S(1)}, f32[128,8,128]{2,1,0:T(8,128)S(1)}, u32[]{:S(2)}, u32[]{:S(2)}) collective-permute-start(f32[128,8,128]{2,1,0:T(8,128)S(1)} %get-tuple-element.289.refs_0_), channel_id=1, source_target_pairs={{0,1},{1,0},{2,3},{3,2},{4,5},{5,4},{6,7},{7,6},{8,9},{9,8},{10,11... | collective-permute-start | bytes 1572872 | tf_op jit(solution)/shard_map/ppermute | solution.py:211
  91.7 7.2 %collective-permute-start.29 = (f32[128,8,128]{2,1,0:T(8,128)S(1)}, f32[128,8,128]{2,1,0:T(8,128)S(1)}, u32[]{:S(2)}, u32[]{:S(2)}) collective-permute-start(f32[128,8,128]{2,1,0:T(8,128)S(1)} %collective-permute-done.28.refs_6_), channel_id=1, source_target_pairs={{0,1},{1,0},{2,3},{3,2},{4,5},{5,4},{6,7},{7,6},{8,9},{9,8},{10,11... | collective-permute-start | bytes 1572872 | tf_op jit(solution)/shard_map/ppermute | solution.py:211
  92.3 13.3 %collective-permute-start.26 = (f32[152,8,128]{2,1,0:T(8,128)S(1)}, f32[152,8,128]{2,1,0:T(8,128)S(1)}, u32[]{:S(2)}, u32[]{:S(2)}) collective-permute-start(f32[152,8,128]{2,1,0:T(8,128)S(1)} %get-tuple-element.288.refs_0_.refs_8_), channel_id=1, source_target_pairs={{0,1},{1,0},{2,3},{3,2},{4,5},{5,4},{6,7},{7,6},{8,9},{9,8},{10,11... | collective-permute-start | bytes 1867784 | tf_op jit(solution)/shard_map/ppermute | solution.py:211
  92.4 13.2 %collective-permute-start.22 = (f32[152,8,128]{2,1,0:T(8,128)S(1)}, f32[152,8,128]{2,1,0:T(8,128)S(1)}, u32[]{:S(2)}, u32[]{:S(2)}) collective-permute-start(f32[152,8,128]{2,1,0:T(8,128)S(1)} %get-tuple-element.288.refs_0_.refs_8_), channel_id=1, source_target_pairs={{0,4},{1,3},{2,6},{3,1},{4,0},{5,7},{6,2},{7,5},{8,12},{9,11},{10,... | collective-permute-start | bytes 1867784 | tf_op jit(solution)/shard_map/ppermute | solution.py:211
  (25 other events, 133.8 us)
